TPU v7x, 32 devices: a whole 2x2x4 slice. The times are simulated.
32 devices in a mesh: wide: 8 (over z, y), narrow: 4 (over x, core).
Axes of the slice: x: 2, y: 2, z: 4, core: 2. Of those that a mesh axis runs over, the one named last changes fastest.
Arguments:
- first_input: bfloat16 [3, 32, 32, 512], P(None, ('wide', 'narrow')), may hold values from -24 to 24
- second_input: bfloat16 [2, 64, 16, 512], P(None, ('wide', 'narrow')), may hold values from -24 to 24
- first_cotangent: bfloat16 [3, 32, 32, 512], P(None, ('wide', 'narrow')), may hold values from -6 to 6
- second_cotangent: bfloat16 [2, 64, 16, 512], P(None, ('wide', 'narrow')), may hold values from -6 to 6
- entry_gain: bfloat16 [512], P('narrow'), may hold values from 0.099609375 to 1.8984375
- entry_shift: bfloat16 [512], P('narrow'), may hold values from -3 to 3
- entry_kernel: bfloat16 [27, 512, 512], P(None, None, 'narrow'), may hold values from -0.0546875 to 0.0546875
- entry_bias: bfloat16 [512], P('narrow'), may hold values from -3 to 3
- exit_gain: bfloat16 [512], P('narrow'), may hold values from 0.099609375 to 1.8984375
- exit_shift: bfloat16 [512], P('narrow'), may hold values from -3 to 3
- exit_kernel: bfloat16 [27, 512, 512], P(None, None, 'narrow'), may hold values from -0.15625 to 0.15625
- exit_bias: bfloat16 [512], P('narrow'), may hold values from -3 to 3
Outputs:
- first_output: bfloat16 [3, 32, 32, 512], P(None, ('wide', 'narrow'))
- second_output: bfloat16 [2, 64, 16, 512], P(None, ('wide', 'narrow'))
- first_input_grad: bfloat16 [3, 32, 32, 512], P(None, ('wide', 'narrow'))
- second_input_grad: bfloat16 [2, 64, 16, 512], P(None, ('wide', 'narrow'))
- entry_gain_grad: float32 [512], P('narrow')
- entry_shift_grad: float32 [512], P('narrow')
- entry_kernel_grad: float32 [27, 512, 512], P(None, None, 'narrow')
- entry_bias_grad: float32 [512], P('narrow')
- exit_gain_grad: float32 [512], P('narrow')
- exit_shift_grad: float32 [512], P('narrow')
- exit_kernel_grad: float32 [27, 512, 512], P(None, None, 'narrow')
- exit_bias_grad: float32 [512], P('narrow')
All inputs are finite; a program needn't handle non-finite values.
Results may differ from a plain program's by a relative error of at most 0.013.
Values may be sent and summed in bfloat16 or wider, within the bound.
A program may use at most 256 MiB of HBM per device.

v0:
```python
import jax
import jax.numpy as jnp
from jax import lax
from jax.sharding import PartitionSpec as P

GROUPS = 32
HEIGHT_ONE = 32
HEIGHT_TWO = 16


epsilon = 1e-06


def extended_2(block, sides, width):
    for axis, dim in sides:
        count = lax.axis_size(axis)
        forward = [(i, i + 1) for i in range(count - 1)]
        backward = [(target, source) for source, target in forward]
        low = lax.ppermute(
            lax.slice_in_dim(block, block.shape[dim] - width, None, axis=dim), axis, forward
        )
        high = lax.ppermute(lax.slice_in_dim(block, 0, width, axis=dim), axis, backward)
        block = jnp.concatenate([low, block, high], axis=dim)
    return block


def swish(values):
    return values * jax.nn.sigmoid(values)


def swish_slope(values):
    sigmoid = jax.nn.sigmoid(values)
    return sigmoid * (1.0 + values * (1.0 - sigmoid))


def band_info(row_count, clip_height):
    position = lax.axis_index(("wide", "narrow")) * row_count
    clip_index = position // clip_height
    top_edge = position % clip_height == 0
    bottom_edge = (position + row_count) % clip_height == 0
    clip_count = lax.axis_size(("wide", "narrow")) * row_count // clip_height
    onehot = (jnp.arange(clip_count, dtype=jnp.int32) == clip_index).astype(jnp.float32)
    return (onehot, top_edge, bottom_edge)


def clear_rims(extended, top_edge, bottom_edge):
    row_count = extended.shape[1]
    row_ids = lax.broadcasted_iota(jnp.int32, (1, row_count, 1, 1), 1)
    masked = jnp.logical_or(
        jnp.logical_and(row_ids == 0, top_edge),
        jnp.logical_and(row_ids == row_count - 1, bottom_edge),
    )
    cleared = jnp.where(masked, jnp.zeros((), extended.dtype), extended)
    return jnp.pad(cleared, ((1, 1), (0, 0), (1, 1), (0, 0)))


def forward_rows(values, top_edge, bottom_edge):
    extended = extended_2(values, ((("wide", "narrow"), 1),), 1)
    return clear_rims(extended, top_edge, bottom_edge)


def backward_rows(values, top_edge, bottom_edge):
    extended = extended_2(values, ((("wide", "narrow"), 1),), 1)
    return clear_rims(extended, top_edge, bottom_edge)


def tap_stack(padded, flipped):
    frame_count = padded.shape[0] - 2
    row_count = padded.shape[1] - 2
    col_count = padded.shape[2] - 2
    pieces = []
    for tap_index in range(27):
        frame_off = tap_index // 9
        row_off = tap_index // 3 % 3
        col_off = tap_index % 3
        pieces.append(
            padded[
                frame_off : frame_off + frame_count,
                row_off : row_off + row_count,
                col_off : col_off + col_count,
            ]
        )
    if flipped:
        pieces = pieces[::-1]
    return jnp.stack(pieces, axis=3).reshape(
        frame_count * row_count * col_count, 27, padded.shape[3]
    )


def apply_kernel(patches, kernel):
    return lax.dot_general(
        patches, kernel, (((1, 2), (0, 1)), ((), ())), preferred_element_type=jnp.float32
    )


def apply_transposed(patches, kernel):
    return lax.dot_general(
        patches, kernel, (((1, 2), (0, 2)), ((), ())), preferred_element_type=jnp.float32
    )


def kernel_grad(patches, grad_rows):
    return lax.dot_general(
        patches, grad_rows, (((0,), (0,)), ((), ())), preferred_element_type=jnp.float32
    )


def pick_clip(onehot, totals):
    return jnp.sum(onehot[:, None] * totals, axis=0)


def normalize(values, onehot, voxel_count):
    grouped = values.reshape(values.shape[0], GROUPS, -1)
    totals = lax.psum(onehot[:, None] * jnp.sum(grouped, axis=(0, 2))[None, :], ("wide", "narrow"))
    group_mean = pick_clip(onehot, totals) / voxel_count
    centered = grouped - group_mean[None, :, None]
    squares = lax.psum(
        onehot[:, None] * jnp.sum(centered * centered, axis=(0, 2))[None, :], ("wide", "narrow")
    )
    variance = pick_clip(onehot, squares) / voxel_count
    inv_std = lax.rsqrt(variance + epsilon)
    return ((centered * inv_std[None, :, None]).reshape(values.shape), inv_std)


def norm_back(grad_norm, normed, inv_std, gain_full, onehot, voxel_count):
    scaled = (grad_norm * gain_full).reshape(grad_norm.shape[0], GROUPS, -1)
    normed_groups = normed.reshape(scaled.shape)
    first_sum, second_sum = lax.psum(
        (
            onehot[:, None] * jnp.sum(scaled, axis=(0, 2))[None, :],
            onehot[:, None] * jnp.sum(scaled * normed_groups, axis=(0, 2))[None, :],
        ),
        ("wide", "narrow"),
    )
    mean_first = pick_clip(onehot, first_sum) / voxel_count
    mean_second = pick_clip(onehot, second_sum) / voxel_count
    result = (
        scaled - mean_first[None, :, None] - normed_groups * mean_second[None, :, None]
    ) * inv_std[None, :, None]
    return result.reshape(grad_norm.shape)


def run_forward(block_input, clip_height, kernel_one, kernel_two, small_params):
    frame_count, row_count, col_count, channels = block_input.shape
    gain_one, shift_one, bias_one, gain_two, shift_two, bias_two = small_params
    onehot, top_edge, bottom_edge = band_info(row_count, clip_height)
    voxel_count = float(frame_count * clip_height * col_count * (channels // GROUPS))
    voxels = frame_count * row_count * col_count
    inputs = block_input.astype(jnp.float32).reshape(voxels, channels)
    normed_one, inv_one = normalize(inputs, onehot, voxel_count)
    hidden_one = normed_one * gain_one + shift_one
    active_one = swish(hidden_one).astype(jnp.bfloat16).reshape(block_input.shape)
    patches_one = tap_stack(forward_rows(active_one, top_edge, bottom_edge), False)
    mid_values = apply_kernel(patches_one, kernel_one) + bias_one
    normed_two, inv_two = normalize(mid_values, onehot, voxel_count)
    hidden_two = normed_two * gain_two + shift_two
    active_two = swish(hidden_two).astype(jnp.bfloat16).reshape(block_input.shape)
    patches_two = tap_stack(forward_rows(active_two, top_edge, bottom_edge), False)
    output = (
        (inputs + apply_kernel(patches_two, kernel_two) + bias_two)
        .astype(jnp.bfloat16)
        .reshape(block_input.shape)
    )
    kept = (
        onehot,
        top_edge,
        bottom_edge,
        voxel_count,
        patches_one,
        normed_one,
        inv_one,
        hidden_one,
        patches_two,
        normed_two,
        inv_two,
        hidden_two,
    )
    return (output, kept)


def run_backward(cotangent, kept, kernel_one, kernel_two, small_params):
    (
        onehot,
        top_edge,
        bottom_edge,
        voxel_count,
        patches_one,
        normed_one,
        inv_one,
        hidden_one,
        patches_two,
        normed_two,
        inv_two,
        hidden_two,
    ) = kept
    gain_one, shift_one, bias_one, gain_two, shift_two, bias_two = small_params
    grid_shape = cotangent.shape
    voxels = patches_one.shape[0]
    grad_rows = cotangent.reshape(voxels, grid_shape[3])
    grad_out = grad_rows.astype(jnp.float32)
    flipped_two = tap_stack(backward_rows(cotangent, top_edge, bottom_edge), True)
    grad_active_two = apply_transposed(flipped_two, kernel_two)
    grad_kernel_two = kernel_grad(patches_two, grad_rows)
    grad_bias_two = jnp.sum(grad_out, axis=0)
    grad_hidden_two = grad_active_two * swish_slope(hidden_two)
    grad_gain_two = jnp.sum(grad_hidden_two * normed_two, axis=0)
    grad_shift_two = jnp.sum(grad_hidden_two, axis=0)
    grad_mid = norm_back(
        grad_hidden_two, normed_two, inv_two, gain_two, onehot, voxel_count
    ).astype(jnp.bfloat16)
    grad_bias_one = jnp.sum(grad_mid.astype(jnp.float32), axis=0)
    flipped_one = tap_stack(
        backward_rows(grad_mid.reshape(grid_shape), top_edge, bottom_edge), True
    )
    grad_active_one = apply_transposed(flipped_one, kernel_one)
    grad_kernel_one = kernel_grad(patches_one, grad_mid)
    grad_hidden_one = grad_active_one * swish_slope(hidden_one)
    grad_gain_one = jnp.sum(grad_hidden_one * normed_one, axis=0)
    grad_shift_one = jnp.sum(grad_hidden_one, axis=0)
    grad_input = grad_out + norm_back(
        grad_hidden_one, normed_one, inv_one, gain_one, onehot, voxel_count
    )
    grad_input = grad_input.astype(jnp.bfloat16).reshape(grid_shape)
    terms = (
        grad_gain_one,
        grad_shift_one,
        grad_kernel_one,
        grad_bias_one,
        grad_gain_two,
        grad_shift_two,
        grad_kernel_two,
        grad_bias_two,
    )
    return (terms, grad_input)


def local(
    first_input,
    second_input,
    first_cotangent,
    second_cotangent,
    entry_gain,
    entry_shift,
    entry_kernel,
    entry_bias,
    exit_gain,
    exit_shift,
    exit_kernel,
    exit_bias,
):
    gathered = (
        lax.all_gather(entry_gain, "narrow", axis=0, tiled=True),
        lax.all_gather(entry_shift, "narrow", axis=0, tiled=True),
        lax.all_gather(entry_kernel, "narrow", axis=2, tiled=True),
        lax.all_gather(entry_bias, "narrow", axis=0, tiled=True),
        lax.all_gather(exit_gain, "narrow", axis=0, tiled=True),
        lax.all_gather(exit_shift, "narrow", axis=0, tiled=True),
        lax.all_gather(exit_kernel, "narrow", axis=2, tiled=True),
        lax.all_gather(exit_bias, "narrow", axis=0, tiled=True),
    )
    gain_one, shift_one, kernel_one, bias_one, gain_two, shift_two, kernel_two, bias_two = gathered
    small_params = tuple(
        (
            param.astype(jnp.float32)
            for param in (gain_one, shift_one, bias_one, gain_two, shift_two, bias_two)
        )
    )
    first_result, first_kept = run_forward(
        first_input, HEIGHT_ONE, kernel_one, kernel_two, small_params
    )
    second_result, second_kept = run_forward(
        second_input, HEIGHT_TWO, kernel_one, kernel_two, small_params
    )
    kernel_one, kernel_two = (
        lax.all_gather(entry_kernel, "narrow", axis=2, tiled=True),
        lax.all_gather(exit_kernel, "narrow", axis=2, tiled=True),
    )
    first_terms, first_back = run_backward(
        first_cotangent, first_kept, kernel_one, kernel_two, small_params
    )
    second_terms, second_back = run_backward(
        second_cotangent, second_kept, kernel_one, kernel_two, small_params
    )
    summed = tuple(
        (left_term + right_term for left_term, right_term in zip(first_terms, second_terms))
    )
    shares = (
        lax.psum_scatter(
            summed[0].astype(jnp.bfloat16), "narrow", scatter_dimension=0, tiled=True
        ).astype(jnp.float32),
        lax.psum_scatter(
            summed[1].astype(jnp.bfloat16), "narrow", scatter_dimension=0, tiled=True
        ).astype(jnp.float32),
        lax.psum_scatter(
            summed[2].astype(jnp.bfloat16), "narrow", scatter_dimension=2, tiled=True
        ).astype(jnp.float32),
        lax.psum_scatter(
            summed[3].astype(jnp.bfloat16), "narrow", scatter_dimension=0, tiled=True
        ).astype(jnp.float32),
        lax.psum_scatter(
            summed[4].astype(jnp.bfloat16), "narrow", scatter_dimension=0, tiled=True
        ).astype(jnp.float32),
        lax.psum_scatter(
            summed[5].astype(jnp.bfloat16), "narrow", scatter_dimension=0, tiled=True
        ).astype(jnp.float32),
        lax.psum_scatter(
            summed[6].astype(jnp.bfloat16), "narrow", scatter_dimension=2, tiled=True
        ).astype(jnp.float32),
        lax.psum_scatter(
            summed[7].astype(jnp.bfloat16), "narrow", scatter_dimension=0, tiled=True
        ).astype(jnp.float32),
    )
    totals = lax.psum(shares, "wide")
    return (
        first_result,
        second_result,
        first_back,
        second_back,
        totals[0],
        totals[1],
        totals[2],
        totals[3],
        totals[4],
        totals[5],
        totals[6],
        totals[7],
    )


def solution(mesh):
    placed = (
        P(None, ("wide", "narrow"), None, None),
        P(None, ("wide", "narrow"), None, None),
        P(None, ("wide", "narrow"), None, None),
        P(None, ("wide", "narrow"), None, None),
        P("narrow"),
        P("narrow"),
        P(None, None, "narrow"),
        P("narrow"),
        P("narrow"),
        P("narrow"),
        P(None, None, "narrow"),
        P("narrow"),
    )
    return jax.shard_map(
        local,
        mesh=mesh,
        in_specs=placed,
        out_specs=(
            P(None, ("wide", "narrow"), None, None),
            P(None, ("wide", "narrow"), None, None),
            P(None, ("wide", "narrow"), None, None),
            P(None, ("wide", "narrow"), None, None),
            P("narrow"),
            P("narrow"),
            P(None, None, "narrow"),
            P("narrow"),
            P("narrow"),
            P("narrow"),
            P(None, None, "narrow"),
            P("narrow"),
        ),
        check_vma=False,
    )
```

profile of v0, /device:TPU:0, one launch (start us, length us, event | category | flops | bytes accessed | tf_op | source)
XLA Modules:
  0.0 1197.9 jit_solution(6353436430629290222)
XLA Ops:
  11.5 45.1 %all-reduce.19 = (f32[1,32]{1,0:T(1,128)S(1)}, f32[4,32]{1,0:T(4,128)S(1)}) all-reduce(f32[1,32]{1,0:T(1,128)S(1)} %multiply_bitcast_fusion.13, f32[4,32]{1,0:T(4,128)S(1)} %broadcast_multiply_fusion.7), channel_id=1, replica_groups=mesh['wide'=8,'narrow'=4] {'wide','narrow'}, use_global_device_ids=true, to_apply=%region_2.3 | all-reduce | flops 160 | bytes 1280 | tf_op jit(solution)/shard_map/psum | solution.py:114
  59.3 41.8 %all-reduce.18 = (f32[1,32]{1,0:T(1,128)S(1)}, f32[4,32]{1,0:T(4,128)S(1)}) all-reduce(f32[1,32]{1,0:T(1,128)S(1)} %multiply_bitcast_fusion.11, f32[4,32]{1,0:T(4,128)S(1)} %broadcast_multiply_fusion.6), channel_id=1, replica_groups=mesh['wide'=8,'narrow'=4] {'wide','narrow'}, use_global_device_ids=true, to_apply=%region_5.6 | all-reduce | flops 160 | bytes 1280 | tf_op jit(solution)/shard_map/psum | solution.py:117
  169.5 8.1 fusion.29
  179.2 44.1 %all-reduce.17 = (f32[1,32]{1,0:T(1,128)S(1)}, f32[4,32]{1,0:T(4,128)S(1)}) all-reduce(f32[1,32]{1,0:T(1,128)S(1)} %multiply_bitcast_fusion.10, f32[4,32]{1,0:T(4,128)S(1)} %broadcast_multiply_fusion.5), channel_id=1, replica_groups=mesh['wide'=8,'narrow'=4] {'wide','narrow'}, use_global_device_ids=true, to_apply=%region_8.9 | all-reduce | flops 160 | bytes 1280 | tf_op jit(solution)/shard_map/psum | solution.py:114
  225.0 41.1 %all-reduce.16 = (f32[1,32]{1,0:T(1,128)S(1)}, f32[4,32]{1,0:T(4,128)S(1)}) all-reduce(f32[1,32]{1,0:T(1,128)S(1)} %multiply_bitcast_fusion.8, f32[4,32]{1,0:T(4,128)S(1)} %broadcast_multiply_fusion.4), channel_id=1, replica_groups=mesh['wide'=8,'narrow'=4] {'wide','narrow'}, use_global_device_ids=true, to_apply=%region_11.12 | all-reduce | flops 160 | bytes 1280 | tf_op jit(solution)/shard_map/psum | solution.py:117
  266.3 11.5 multiply_reduce_fusion
  278.4 10.5 multiply_reduce_fusion.8
  289.4 39.1 %all-reduce.15 = (f32[1,32]{1,0:T(1,128)S(1)}, f32[1,32]{1,0:T(1,128)S(1)}, f32[4,32]{1,0:T(4,128)S(1)}, f32[4,32]{1,0:T(4,128)S(1)}) all-reduce(f32[1,32]{1,0:T(1,128)S(1)} %multiply_bitcast_fusion.5, f32[1,32]{1,0:T(1,128)S(1)} %multiply_bitcast_fusion.7, ...), channel_id=1, replica_groups=mesh['wide'=8,'narrow'=4] {'wide','narrow'}, use_global_device_ids=true, to_apply=%region_33.34 | all-reduce | flops 320 | bytes 2560 | tf_op jit(solution)/shard_map/psum | solution.py:128
  333.9 11.4 fusion.20
  345.4 17.0 %add_convert_fusion = bf16[27,512,512]{2,1,0:T(8,128)(2,1)} fusion(f32[27,512,512]{2,1,0:T(8,128)} %fusion.20, bf16[64,27,512]{2,0,1:T(8,128)(2,1)} %copy-done, bf16[64,512]{1,0:T(8,128)(2,1)S(1)} %get-tuple-element.111), kind=kOutput, calls=%fused_computation.2 | convolution fusion | flops 920125440 | bytes 44302336 | tf_op jit(solution)/shard_map/dot_general | solution.py:103
  362.3 28.0 %copy.103 = bf16[27,512,512]{1,0,2:T(8,128)(2,1)} copy(bf16[27,512,512]{2,1,0:T(8,128)(2,1)} %add_convert_fusion) | data formatting | bytes 28311552
  390.3 15.2 %copy.107 = bf16[64,8,27,512]{3,1,2,0:T(8,128)(2,1)} copy(bf16[64,8,27,512]{3,2,1,0:T(8,128)(2,1)} %bitcast.571) | data formatting | bytes 28311552
  429.7 12.2 %fusion.1 = f32[27,512,512,1]{2,1,3,0:T(8,128)} fusion(bf16[3,1,32,27,512]{4,2,0,3,1:T(8,128)(2,1)S(1)} %constant_dynamic-update-slice_fusion.216, bf16[3,1,32,512]{3,2,1,0:T(8,128)(2,1)S(1)} %copy-done.4), kind=kOutput, calls=%fused_computation.3 | convolution fusion | flops 1358954496 | bytes 31064064 | tf_op jit(solution)/shard_map/dot_general | solution.py:103
  441.9 17.5 %fusion = bf16[27,512,512]{2,1,0:T(8,128)(2,1)} fusion(f32[27,512,512,1]{2,1,3,0:T(8,128)} %fusion.1, bf16[2,2,16,27,512]{4,2,1,3,0:T(8,128)(2,1)} %copy-done.31, bf16[2,2,16,512]{3,2,1,0:T(8,128)(2,1)S(1)} %copy-done.5), kind=kOutput, calls=%fused_computation.1 | convolution fusion | flops 920125440 | bytes 44302336 | tf_op jit(solution)/shard_map/dot_general | solution.py:103
  459.4 28.1 %copy.105 = bf16[27,512,512]{1,0,2:T(8,128)(2,1)} copy(bf16[27,512,512]{2,1,0:T(8,128)(2,1)} %fusion) | data formatting | bytes 28311552
  487.6 15.2 %copy.108 = bf16[64,8,27,512]{3,1,2,0:T(8,128)(2,1)} copy(bf16[64,8,27,512]{3,2,1,0:T(8,128)(2,1)} %bitcast.572) | data formatting | bytes 28311552
  503.4 9.3 all-gather.5
  514.9 10.2 multiply_reduce_fusion.9
  527.4 11.5 fusion.14
  539.6 9.7 multiply_reduce_fusion.1
  549.8 45.7 %all-reduce.14 = (f32[1,32]{1,0:T(1,128)S(1)}, f32[1,32]{1,0:T(1,128)S(1)}, f32[4,32]{1,0:T(4,128)S(1)}, f32[4,32]{1,0:T(4,128)S(1)}) all-reduce(f32[1,32]{1,0:T(1,128)S(1)} %multiply_bitcast_fusion.1, f32[1,32]{1,0:T(1,128)S(1)} %multiply_bitcast_fusion.3, ...), channel_id=1, replica_groups=mesh['wide'=8,'narrow'=4] {'wide','narrow'}, use_global_device_ids=true, to_apply=%region_39.40 | all-reduce | flops 320 | bytes 2560 | tf_op jit(solution)/shard_map/psum | solution.py:128
  608.7 8.2 fusion.8
  636.5 7.8 copy.106
  644.3 546.5 %all-reduce.23 = (f32[128]{0:T(128)}, f32[128]{0:T(128)}, f32[27,512,128]{2,1,0:T(8,128)}, f32[128]{0:T(128)}, f32[128]{0:T(128)}, /*index=5*/f32[128]{0:T(128)}, f32[27,512,128]{2,1,0:T(8,128)}, f32[128]{0:T(128)}) all-reduce(f32[128]{0:T(128)S(1)} %dynamic-slice_convert_fusion.5, ...), channel_id=1, replica_groups=mesh['wide'=8,'narrow'=4] {'wide'}, use_global_device_ids=true, to_apply=%region_59.60 | all-reduce | flops 3539712 | bytes 21239808 | tf_op jit(solution)/shard_map/psum | solution.py:313
  (579 shorter events, 145.0 us)
Async XLA Ops:
  7.2 153.9 %all-gather.9.cloned.1.call-start = ((), (), s32[]{:S(2)}) async-start(), calls=%async_computation.2 | async-start | bytes 17694720 | tf_op jit(solution)/shard_map/all_gather | solution.py:254
  8.0 116.1 %copy-start.44 = (bf16[128]{0:T(256)(128)(2,1)S(1)}, bf16[128]{0:T(256)(128)(2,1)}, u32[]{:S(2)}) copy-start(bf16[128]{0:T(256)(128)(2,1)} %param.20) | copy-start | bytes 772
  8.0 121.1 %copy-start.45 = (bf16[128]{0:T(256)(128)(2,1)S(1)}, bf16[128]{0:T(256)(128)(2,1)}, u32[]{:S(2)}) copy-start(bf16[128]{0:T(256)(128)(2,1)} %param.21) | copy-start | bytes 772
  8.0 258.2 %all-gather.11.cloned.1.call-start = ((), (), s32[]{:S(2)}) async-start(), calls=%async_computation.3 | async-start | bytes 17694720 | tf_op jit(solution)/shard_map/all_gather | solution.py:258
  8.1 134.4 %collective-permute-start.9 = (bf16[3,1,32,512]{3,2,0,1:T(8,128)(2,1)S(1)}, bf16[3,1,32,512]{3,2,0,1:T(8,128)(2,1)S(1)}, u32[]{:S(2)}, u32[]{:S(2)}) collective-permute-start(bf16[3,1,32,512]{3,2,0,1:T(8,128)(2,1)S(1)} %bitcast.578), channel_id=1, source_target_pairs={{1,0},{2,1},{3,2},{4,3},{5,4},{6,5},{7,6},{8,7},{9,8},{10,9},{11,1... | collective-permute-start | bytes 294920 | tf_op jit(solution)/shard_map/ppermute | solution.py:22
  9.5 607.4 %reduce-scatter.7.cloned.1.call-start = ((), (), s32[]{:S(2)}) async-start(), calls=%async_computation.4 | async-start | bytes 17694720
  10.2 124.0 %collective-permute-start.13 = (bf16[2,1,16,512]{3,2,1,0:T(8,128)(2,1)S(1)}, bf16[2,1,16,512]{3,2,1,0:T(8,128)(2,1)S(1)}, u32[]{:S(2)}, u32[]{:S(2)}) collective-permute-start(bf16[2,1,16,512]{3,2,1,0:T(8,128)(2,1)S(1)} %get-tuple-element.335), channel_id=1, source_target_pairs={{1,0},{2,1},{3,2},{4,3},{5,4},{6,5},{7,6},{8,7},{9,8},{10,9},{11,1... | collective-permute-start | bytes 98312 | tf_op jit(solution)/shard_map/ppermute | solution.py:22
  57.6 78.8 %collective-permute-start.12 = (bf16[2,1,16,512]{3,2,1,0:T(8,128)(2,1)S(1)}, bf16[2,1,16,512]{3,2,1,0:T(8,128)(2,1)S(1)}, u32[]{:S(2)}, u32[]{:S(2)}) collective-permute-start(bf16[2,1,16,512]{3,2,1,0:T(8,128)(2,1)S(1)} %get-tuple-element.334), channel_id=1, source_target_pairs={{0,1},{1,2},{2,3},{3,4},{4,5},{5,6},{6,7},{7,8},{8,9},{9,10},{10,1... | collective-permute-start | bytes 98312 | tf_op jit(solution)/shard_map/ppermute | solution.py:19
  112.2 25.5 %collective-permute-start.5 = (bf16[2,1,16,512]{3,2,1,0:T(8,128)(2,1)S(1)}, bf16[2,1,16,512]{3,2,1,0:T(8,128)(2,1)S(1)}, u32[]{:S(2)}, u32[]{:S(2)}) collective-permute-start(bf16[2,1,16,512]{3,2,1,0:T(8,128)(2,1)S(1)} %get-tuple-element.339), channel_id=1, source_target_pairs={{1,0},{2,1},{3,2},{4,3},{5,4},{6,5},{7,6},{8,7},{9,8},{10,9},{11,1... | collective-permute-start | bytes 98312 | tf_op jit(solution)/shard_map/ppermute | solution.py:22
  113.5 27.7 %collective-permute-start.4 = (bf16[2,1,16,512]{3,2,1,0:T(8,128)(2,1)S(1)}, bf16[2,1,16,512]{3,2,1,0:T(8,128)(2,1)S(1)}, u32[]{:S(2)}, u32[]{:S(2)}) collective-permute-start(bf16[2,1,16,512]{3,2,1,0:T(8,128)(2,1)S(1)} %get-tuple-element.338), channel_id=1, source_target_pairs={{0,1},{1,2},{2,3},{3,4},{4,5},{5,6},{6,7},{7,8},{8,9},{9,10},{10,1... | collective-permute-start | bytes 98312 | tf_op jit(solution)/shard_map/ppermute | solution.py:19
  129.1 137.2 %copy-start.14 = (f32[4,1,128]{2,1,0:T(1,128)}, f32[4,1,128]{2,1,0:T(1,128)S(1)}, u32[]{:S(2)}) copy-start(f32[4,1,128]{2,1,0:T(1,128)S(1)} %convert_element_type.198) | copy-start | bytes 6148
  134.1 132.1 %copy-start.16 = (f32[4,1,128]{2,1,0:T(1,128)}, f32[4,1,128]{2,1,0:T(1,128)S(1)}, u32[]{:S(2)}) copy-start(f32[4,1,128]{2,1,0:T(1,128)S(1)} %convert_element_type.199) | copy-start | bytes 6148
  134.2 8.3 collective-permute-start.8
  136.4 6.1 collective-permute-start.1
  137.7 6.0 collective-permute-start
  405.5 224.6 %reduce-scatter.9.cloned.1.call-start = ((), (), s32[]{:S(2)}) async-start(), calls=%async_computation.5 | async-start | bytes 17694720
  405.6 11.6 collective-permute-start.15
  406.9 14.6 %collective-permute-start.14 = (bf16[2,1,16,512]{3,2,1,0:T(8,128)(2,1)S(1)}, bf16[2,1,16,512]{3,2,1,0:T(8,128)(2,1)S(1)}, u32[]{:S(2)}, u32[]{:S(2)}) collective-permute-start(bf16[2,1,16,512]{3,2,1,0:T(8,128)(2,1)S(1)} %get-tuple-element.332), channel_id=1, source_target_pairs={{0,1},{1,2},{2,3},{3,4},{4,5},{5,6},{6,7},{7,8},{8,9},{9,10},{10,1... | collective-permute-start | bytes 98312 | tf_op jit(solution)/shard_map/ppermute | solution.py:19
  409.9 12.8 %collective-permute-start.7 = (bf16[2,1,16,512]{3,2,1,0:T(8,128)(2,1)S(1)}, bf16[2,1,16,512]{3,2,1,0:T(8,128)(2,1)S(1)}, u32[]{:S(2)}, u32[]{:S(2)}) collective-permute-start(bf16[2,1,16,512]{3,2,1,0:T(8,128)(2,1)S(1)} %get-tuple-element.337), channel_id=1, source_target_pairs={{1,0},{2,1},{3,2},{4,3},{5,4},{6,5},{7,6},{8,7},{9,8},{10,9},{11,1... | collective-permute-start | bytes 98312 | tf_op jit(solution)/shard_map/ppermute | solution.py:22
  411.5 15.6 %collective-permute-start.6 = (bf16[2,1,16,512]{3,2,1,0:T(8,128)(2,1)S(1)}, bf16[2,1,16,512]{3,2,1,0:T(8,128)(2,1)S(1)}, u32[]{:S(2)}, u32[]{:S(2)}) collective-permute-start(bf16[2,1,16,512]{3,2,1,0:T(8,128)(2,1)S(1)} %get-tuple-element.336), channel_id=1, source_target_pairs={{0,1},{1,2},{2,3},{3,4},{4,5},{5,6},{6,7},{7,8},{8,9},{9,10},{10,1... | collective-permute-start | bytes 98312 | tf_op jit(solution)/shard_map/ppermute | solution.py:19
  415.9 11.9 collective-permute-start.11
  417.2 10.6 collective-permute-start.10
  421.5 6.3 collective-permute-start.3
  422.8 6.2 collective-permute-start.2
  (44 other events, 784.9 us)
Sparse Core Ops, SparseCore 0:
  9.6 98.2 all-gather.8
  109.5 96.8 all-gather.10
  405.6 110.2 reduce-scatter.6
  518.4 111.1 reduce-scatter.8
where the time goes:
time: 1210 us; the launch traced here: 1200 us
  blocking collectives  847 us (70%)
  local copies, waits for them, and re-layouts  146 us (12%)
  matrix products  135 us (11%)
  starting transfers between devices  37.2 us (3%)
  between operations  18 us (1%)
  other arithmetic  13 us (1%)
    psum x1, blocking collectives, local(): totals = lax.psum(shares, 'wide')  547 us
    unnamed x365, local copies, waits for them, and re-layouts  137 us
    psum x2, blocking collectives, normalize(): lax.psum(onehot[:, None] * jnp.sum(grouped, axis=(0, 2))[None, :], ('wide...  89.2 us
    psum x2, blocking collectives, norm_back(): lax.psum((onehot[:, None] * jnp.sum(scaled, axis=(0, 2))[None, :], onehot...  84.8 us
    psum x2, blocking collectives, normalize(): lax.psum(onehot[:, None] * jnp.sum(centered * centered, axis=(0, 2))[None...  82.9 us
    dot_general x4, matrix products, kernel_grad(): lax.dot_general(patches, grad_rows, (((0,), (0,)), ((), ())), preferred_e...  58 us
    dot_general x4, matrix products, apply_transposed(): lax.dot_general(patches, kernel, (((1, 2), (0, 2)), ((), ())), preferred_...  41.9 us
    dot_general x4, matrix products, apply_kernel(): lax.dot_general(patches, kernel, (((1, 2), (0, 1)), ((), ())), preferred_...  35.5 us
  transfers between devices with their start and end apart: 20, of which 0 were waited for; matrix products, arithmetic and copies ran while one was open for 15% of the time, Pallas kernels for 0%

commit v1 on v0

v1 whole, which is shorter than its diff:
```python
import functools

import jax
import jax.numpy as jnp
from jax import lax
from jax.experimental import pallas as pl
from jax.experimental.pallas import tpu as pltpu
from jax.sharding import PartitionSpec as P

GROUPS = 32
HEIGHT_ONE = 32
HEIGHT_TWO = 16
CHANNELS = 512
NARROW = 4
BANDS = 8
SLICE = 128
FRAMES = 5
FIRST = 3
BAND = 128
OWN = 32
LONG = 192

EPS = 1e-06
F32 = jnp.float32
BF16 = jnp.bfloat16
MESH = pl.DeviceIdType.MESH

FORWARD = {
    1: ((0, 3, 0), (3, 5, 3)),
    0: ((0, 2, 1), (3, 4, 4)),
    2: ((1, 3, 0), (4, 5, 3)),
}
BACKWARD = {
    1: ((0, 3, 0), (3, 5, 3)),
    0: ((1, 3, 0), (4, 5, 3)),
    2: ((0, 2, 1), (3, 4, 4)),
}


TWO = {"x": True, "a2": False}
ORDER = (
    "prep",
    "st0",
    "xh1",
    "gown",
    "gstart",
    "xsend",
    "xh2",
    "T2",
    "T2b",
    "z g 1",
    "xown",
    "act",
    "T2c",
    "C1",
    "z g 2",
    "C1b",
    "C1c",
    "rs0",
    "S2",
    "a2start",
    "z g 3",
    "padg 0",
    "z a2 1",
    "padg 1",
    "gh2",
    "S3",
    "padg 2",
    "a2own",
    "padg 3",
    "y a2 0",
    "xbulk",
    "T1",
    "y a2 1",
    "o a2 0 1",
    "T1b",
    "o a2 1 0",
    "z a2 2",
    "prepa 0",
    "wx 0 0 0",
    "wx 0 0 1",
    "wx 0 0 2",
    "wx 0 0 3",
    "wx 0 0 4",
    "z x 1",
    "T1c",
    "wx 0 1 0",
    "z a2 3",
    "wx 0 1 1",
    "wx 0 1 2",
    "wx 0 1 3",
    "wx 0 1 4",
    "wx 0 2 0",
    "wx 0 2 1",
    "wx 0 2 2",
    "o a2 1 1",
    "y a2 2",
    "wx 0 2 3",
    "wx 0 2 4",
    "mstart",
    "o a2 2 0",
    "prepa 1",
    "wx 1 0 0",
    "wx 1 0 1",
    "wx 1 0 2",
    "wx 1 0 3",
    "rt",
    "wx 1 0 4",
    "wx 1 1 0",
    "wx 1 1 1",
    "wx 1 1 2",
    "wx 1 1 3",
    "z x 2",
    "y a2 3",
    "wx 1 1 4",
    "wx 1 2 0",
    "wx 1 2 1",
    "o a2 2 1",
    "y x 0",
    "wx 1 2 2",
    "wx 1 2 3",
    "wx 1 2 4",
    "y x 1",
    "prepa 2",
    "wx 2 0 0",
    "C2",
    "wx 2 0 1",
    "z m 1",
    "wx 2 0 2",
    "o a2 3 0",
    "wx 2 0 3",
    "wx 2 0 4",
    "wx 2 1 0",
    "wx 2 1 1",
    "padm 0",
    "wx 2 1 2",
    "wx 2 1 3",
    "wx 2 1 4",
    "z x 3",
    "wx 2 2 0",
    "wx 2 2 1",
    "wx 2 2 2",
    "wx 2 2 3",
    "wx 2 2 4",
    "y x 2",
    "o a2 3 1",
    "z m 2",
    "C2b",
    "gh1",
    "o x 1 1",
    "C2c",
    "prepa 3",
    "wx 3 0 0",
    "wx 3 0 1",
    "y x 3",
    "o x 0 1",
    "z m 3",
    "wx 3 0 2",
    "S4",
    "wx 3 0 3",
    "wx 3 0 4",
    "wx 3 1 0",
    "wx 3 1 1",
    "wx 3 1 2",
    "wx 3 1 3",
    "o x 2 1",
    "padm 1",
    "wx 3 1 4",
    "wx 3 2 0",
    "wx 3 2 1",
    "padm 2",
    "prepx 0",
    "prepx 1",
    "prepx 2",
    "o x 3 1",
    "wx 3 2 2",
    "wx 3 2 3",
    "out",
    "wx 3 2 4",
    "S5",
    "padm 3",
    "prepx 3",
    "fin",
)
REAPS = (47, 71, 94, 118, 136)


def sigmoid_of(values):
    return 0.5 * jnp.tanh(0.5 * values) + 0.5


def group_sum(tile):
    lanes = lax.broadcasted_iota(jnp.int32, tile.shape, 1)
    for step in (1, 2, 4, 8):
        up = pltpu.roll(tile, step, 1)
        down = pltpu.roll(tile, SLICE - step, 1)
        tile = tile + jnp.where((lanes & step) != 0, up, down)
    return tile


def column_ids(rows, width):
    return lax.broadcasted_iota(jnp.int32, (rows, SLICE), 0) % width


def shifted(values, width, k):
    if k == 1:
        return values
    rows = values.shape[0]
    cols = column_ids(rows, width)
    if k == 0:
        return jnp.where(cols == width - 1, 0.0, pltpu.roll(values, rows - 1, 0))
    return jnp.where(cols == 0, 0.0, pltpu.roll(values, 1, 0))


def three_shifts(values, width):
    wide = values.astype(F32)
    return jnp.concatenate([shifted(wide, width, k).astype(BF16) for k in range(3)], axis=1)


def taken(ref, spans, start_one, start_two):
    (a, b, _), (c, d, _) = spans
    one = ref[a:b, start_one : start_one + BAND, :]
    two = ref[c:d, start_two : start_two + BAND, :]
    lanes = ref.shape[2]
    return jnp.concatenate(
        [one.reshape((b - a) * BAND, lanes), two.reshape((d - c) * BAND, lanes)], axis=0
    )


def spread(out, spans, result, fresh):
    (a, b, o), (c, d, p) = spans
    cut = (b - a) * BAND
    one = result[:cut].reshape(b - a, BAND, -1)
    two = result[cut:].reshape(d - c, BAND, -1)
    if fresh:
        out[o : o + b - a] = one
        out[p : p + d - c] = two
    else:
        out[o : o + b - a] += one
        out[p : p + d - c] += two


PARTS = (1, 0, 2)


def conv_forward(act, weights, sums, part):
    i = PARTS[part]
    spans = FORWARD[i]
    rows = jnp.concatenate([taken(act, spans, 32 * j, 16 + 16 * j) for j in range(3)], axis=1)
    taps = weights[3 * i : 3 * i + 3].reshape(3 * CHANNELS, 3 * SLICE)
    spread(sums, spans, jnp.dot(rows, taps, preferred_element_type=F32), part == 0)


def conv_columns(sums, frame, width):
    total = sums[frame, :, SLICE : 2 * SLICE]
    total = total + shifted(sums[frame, :, 0:SLICE], width, 2)
    return total + shifted(sums[frame, :, 2 * SLICE : 3 * SLICE], width, 0)


def conv_backward(grads, weights, sums, part):
    i = PARTS[part]
    spans = BACKWARD[i]
    rows = jnp.concatenate(
        [taken(grads, spans, 64 - 32 * j, 48 - 16 * j) for j in range(3)], axis=1
    )
    taps = jnp.concatenate([weights[3 * i + j] for j in range(3)], axis=1)
    result = lax.dot_general(rows, taps, (((1,), (1,)), ((), ())), preferred_element_type=F32)
    spread(sums, spans, result, part == 0)


def moments(values):
    total = jnp.sum(values, axis=0, keepdims=True)
    off = values - total / values.shape[0]
    return total, jnp.sum(off * off, axis=0, keepdims=True)


def merge(totals, squares, count):
    total = functools.reduce(jnp.add, totals)
    mean = total / (count * len(totals))
    square = functools.reduce(jnp.add, squares)
    for part in totals:
        off = part / count - mean
        square = square + count * off * off
    return total, square


def group_merge(total, square, count):
    mean = total / count
    group_total = group_sum(total)
    off = mean - group_total / (16 * count)
    return group_total, group_sum(square + count * off * off)


def long_row(tile, row):
    return jnp.concatenate([tile[row + k : row + k + 1, :] for k in range(NARROW)], axis=1)


def lanes_of(m):
    if isinstance(m, int):
        return pl.ds(m * SLICE, SLICE)
    return pl.ds(pl.multiple_of(m * SLICE, SLICE), SLICE)


def place_of(k):
    return k % 2 * 2 + k // 2


def store_taps(out, taps, result, fresh):
    for number, tap in enumerate(taps):
        for k in range(NARROW):
            start = place_of(k) * SLICE
            piece = result[start : start + SLICE, number * SLICE : (number + 1) * SLICE]
            rows = slice(k * SLICE, (k + 1) * SLICE)
            if fresh:
                out[tap, rows, :] = piece
            else:
                out[tap, rows, :] += piece


def rows_of(m, offset=0):
    return pl.ds(pl.multiple_of(offset + m * OWN, OWN), OWN)


def clear_pads(three_one, three_two):
    for start in (0, three_one.shape[1] - 32):
        three_one[:, start : start + 32, :] = jnp.zeros((FIRST, 32, 3 * SLICE), BF16)
    for start in (0, three_two.shape[2] - 16):
        three_two[:, :, start : start + 16, :] = jnp.zeros((FRAMES - FIRST, 4, 16, 3 * SLICE), BF16)


def pad_pair(grad_ref, three_one, three_two, pair):
    @pl.loop(0, 2)
    def _(half):
        first = pl.multiple_of(half * BAND, BAND)

        @pl.loop(0, FIRST)
        def _(f):
            start = pl.multiple_of(32 + pair * 2 * BAND + first, 32)
            three_one[f, pl.ds(start, BAND), :] = three_shifts(grad_ref[2 * pair + half, f], 32)

        @pl.loop(0, FRAMES - FIRST)
        def _(f):
            start = pl.multiple_of(16 + first, 16)
            three_two[f, pair, pl.ds(start, BAND), :] = three_shifts(grad_ref[2 * pair + half, FIRST + f], 16)


PAIRS = {
    0: ((0, 1), (1, 2), (3, 4)),
    1: ((0, 0), (1, 1), (2, 2), (3, 3), (4, 4)),
    2: ((1, 0), (2, 1), (4, 3)),
}
TAP_GROUPS = ((0, 1), (2, 3), (4, 5), (6, 7), (8,))


def tap_rows(three_one, three_two, t, tap):
    j, k = tap // 3, tap % 3
    cut = slice(k * SLICE, (k + 1) * SLICE)
    if t < FIRST:
        return three_one[t, (2 - j) * 32 : (2 - j) * 32 + 1024, cut]
    return three_two[t - FIRST, :, (2 - j) * 16 : (2 - j) * 16 + 256, cut].reshape(1024, SLICE)


def weight_terms(act_t, three_one, three_two, i, pairs, group, out, fresh):
    left = jnp.concatenate([act_t[c, s] for s, _ in pairs for c in range(BANDS)], axis=1)
    right = jnp.concatenate(
        [
            jnp.concatenate([tap_rows(three_one, three_two, t, tap) for tap in group], axis=1)
            for _, t in pairs
        ],
        axis=0,
    )
    result = jnp.dot(left, right, preferred_element_type=F32)
    store_taps(out, [9 * i + tap for tap in group], result, fresh)


def pair_weight_terms(act_t, three_one, three_two, pair, i, group, out, fresh):
    def rows(t, tap):
        j, cut = tap // 3, slice(tap % 3 * SLICE, (tap % 3 + 1) * SLICE)
        if t < FIRST:
            start = pl.multiple_of((2 - j) * 32 + pair * 2 * BAND, 32)
            return three_one[t, pl.ds(start, 2 * BAND), cut]
        return three_two[t - FIRST, pair, (2 - j) * 16 : (2 - j) * 16 + 2 * BAND, cut]

    left = jnp.concatenate([act_t[2 * pair + half, s] for s, _ in PAIRS[i] for half in range(2)], axis=1)
    right = jnp.concatenate(
        [jnp.concatenate([rows(t, tap) for tap in group], axis=1) for _, t in PAIRS[i]], axis=0
    )
    result = jnp.dot(left, right, preferred_element_type=F32)
    store_taps(out, [9 * i + tap for tap in group], result, fresh)


def block_kernel(
    x_one, x_two, g_one, g_two, gain_one, shift_one, bias_one, gain_two, shift_two, bias_two,
    entry_hbm, exit_hbm,
    out_one, out_two, back_one, back_two, smalls, act_out, wide_one_out, wide_two_out, exit_grad,
    act_t1, act_t2, g_all, gm_all, three_one, three_two, wide_one, wide_two, exit_sum,
    entry_w, exit_w, own_x, own_g, band_x, band_a, long_g, long_m, params,
    stat_a, stat_b, stat_c, stat_d, stat_e, stat_f, few,
    sums, partial, grad_three, mid, grad_two, grad_one, part_send, part_recv, tail_send, tail_recv, out_send,
    w_sem, send_sem, x_sem, g_sem, p_sem, halo_sem, stat_sem, ga_sem, gm_sem, a1_sem, a2_sem, rs_sem, o_sem, store_sem,
):
    w = lax.axis_index("wide")
    n = lax.axis_index("narrow")
    base = w // BANDS * BANDS
    b = w - base
    z, y = b // 2, b % 2
    has_up, has_down = b > 0, b < BANDS - 1
    pair_up, pair_down = y == 1, y == 0
    flags = lambda f: (has_up, has_down) if f < FIRST else (pair_up, pair_down)
    width_of = lambda f: 32 if f < FIRST else 16
    sub_of = lambda f: 0 if f < FIRST else 1

    sends = []
    used = [0]

    def both(first, second):
        if first is None or second is None:
            return second if first is None else first
        return jnp.logical_and(first, second)

    def under(flag, act):
        if flag is None:
            act()
        else:
            pl.when(flag)(act)

    def make(src, dst, recv, device):
        used[0] += 1
        return pltpu.make_async_remote_copy(
            src_ref=src,
            dst_ref=dst,
            send_sem=send_sem.at[used[0] - 1],
            recv_sem=recv,
            device_id=device,
            device_id_type=MESH,
        )

    def start(copies):
        for copy in copies:
            copy.start()

    def launch(copies, flag=None):
        under(flag, lambda: start(copies))
        sends.append((flag, copies))

    def send(src, dst, recv, device, flag=None):
        launch([make(src, dst, recv, device)], flag)

    def reap(count):
        for flag, copies in sends[:count]:

            def wait_all(copies=copies):
                for copy in copies:
                    copy.wait_send()

            under(flag, wait_all)
        del sends[:count]

    def arrived(dst, recv, flag=None):
        wait = pltpu.make_async_remote_copy(
            src_ref=dst,
            dst_ref=dst,
            send_sem=send_sem.at[0],
            recv_sem=recv,
            device_id=(w, n),
            device_id_type=MESH,
        ).wait_recv
        under(flag, wait)

    def beside(m):
        return (w, m)

    def band_of(c):
        return (base + c, n)

    others = [lax.rem(n + d, NARROW) for d in (1, 2, 3)]
    far = [lax.rem(b + d, BANDS) for d in range(1, BANDS)]
    sib, opp, cross = n ^ 1, n ^ 2, n ^ 3
    beyond = b + 1 - 2 * y
    slant = b - 1 + 2 * y
    above = lax.rem(b + BANDS - 1, BANDS)
    below = lax.rem(b + 1, BANDS)
    up_chip = lax.rem(b + BANDS - 2, BANDS)
    down_chip = lax.rem(b + 2, BANDS)
    pairs_by_distance = [z, z + 1 - 2 * (z % 2), 2 - z // 2, 3 - 3 * (z // 2)]
    mine, mine_long = rows_of(n), rows_of(n, 32)

    sem_of = {"x": a1_sem, "a2": a2_sem, "g": ga_sem, "m": gm_sem}
    array_of = {"x": act_t1, "a2": act_t2, "g": g_all, "m": gm_all}

    def block(name, c, k):
        if name in ("g", "m"):
            return array_of[name].at[c]
        return array_of[name].at[c, :, lanes_of(place_of(k)), :]

    def couple(name, c, k):
        rows = pl.ds(pl.multiple_of(k % 2 * 2 * SLICE, 2 * SLICE), 2 * SLICE)
        return array_of[name].at[c, :, rows, :]

    def sem(name, c, kind):
        return sem_of[name].at[c] if name in ("g", "m") else sem_of[name].at[c, kind]

    def own(name, c):
        return couple(name, c, n) if TWO.get(name) else block(name, c, n)

    def to(ref, name, c, kind, device):
        return make(ref, ref, sem(name, c, kind), device)

    def to_opp(name, c):
        return to(block(name, c, n), name, c, 1, beside(opp))

    def to_sib(name, c):
        return to(couple(name, c, n), name, c, 2, beside(sib))

    def to_beyond(name, c):
        return to(block(name, c, n), name, c, 0, band_of(beyond))

    def at_distance(step, line):
        for sign in (-1, 1) if step else (1,):
            there = None if step == 0 else (z >= step if sign < 0 else z + step <= 3)
            c = lax.rem(b + 2 * sign * step + BANDS, BANDS)
            yield sign, there, c if line == 0 else c + 1 - 2 * y

    def z_step(name, step):
        for sign, there, c in at_distance(step, 0):
            arrived(own(name, c), sem(name, c, 0), there)
            copies = [to_beyond(name, c)]
            if name in ("x", "a2"):
                copies.append(to_sib(name, c) if TWO[name] else to_opp(name, c))
            if step < 3:
                onward, target = (z < 3, down_chip) if sign < 0 else (z > 0, up_chip)
                launch([to(own(name, c), name, c, 0, band_of(target))], both(there, onward))
            launch(copies, there)

    def y_step(name, step):
        for _, there, c in at_distance(step, 1):
            arrived(block(name, c, n), sem(name, c, 0), there)
            launch([to_opp(name, c)], there)

    def o_step(name, step, line):
        for _, there, c in at_distance(step, line):
            arrived(block(name, c, opp), sem(name, c, 1), there)
            launch([to_sib(name, c)], there)

    def begin(name):
        launch([to(own(name, b), name, b, 0, band_of(down_chip))], z < 3)
        launch([to(own(name, b), name, b, 0, band_of(up_chip))], z > 0)
        launch([to_beyond(name, b)])

    def await_sib(name, c):
        arrived(couple(name, c, sib), sem(name, c, 2))

    def to_bands(stat, number):
        for c in far:
            send(stat.at[b], stat.at[b], stat_sem.at[number, b], band_of(c))

    def from_bands(stat, number):
        for c in far:
            arrived(stat.at[b], stat_sem.at[number, c])

    def to_narrow(stat, number):
        for m in others:
            send(stat.at[n], stat.at[n], stat_sem.at[number, n], beside(m))

    def from_narrow(stat, number):
        for m in others:
            arrived(stat.at[n], stat_sem.at[number, m])

    def exchange_rims(ref, first_sem):
        send(ref.at[0:3, 128:160, :], ref.at[0:3, 0:32, :], halo_sem.at[first_sem], band_of(below), has_down)
        send(ref.at[0:3, 32:64, :], ref.at[0:3, 160:192, :], halo_sem.at[first_sem + 1], band_of(above), has_up)
        send(ref.at[3:5, 144:160, :], ref.at[3:5, 16:32, :], halo_sem.at[first_sem + 2], band_of(beyond), pair_down)
        send(ref.at[3:5, 32:48, :], ref.at[3:5, 160:176, :], halo_sem.at[first_sem + 3], band_of(beyond), pair_up)

    def await_rims(ref, first_sem):
        arrived(ref.at[0:3, 0:32, :], halo_sem.at[first_sem], has_up)
        arrived(ref.at[0:3, 160:192, :], halo_sem.at[first_sem + 1], has_down)
        arrived(ref.at[3:5, 16:32, :], halo_sem.at[first_sem + 2], pair_up)
        arrived(ref.at[3:5, 160:176, :], halo_sem.at[first_sem + 3], pair_down)

    kept = {}
    count_one = 3 * BAND * BANDS
    count_two = 2 * BAND * 2

    def prep():
        loads = []
        for number, (source, target) in enumerate(((exit_hbm, exit_w), (entry_hbm, entry_w))):
            for k in range(3):
                load = pltpu.make_async_copy(
                    source.at[:, k],
                    target.at[:, :, k * SLICE : (k + 1) * SLICE],
                    w_sem.at[number, k],
                )
                load.start()
                loads.append(load)
        kept["loads"] = loads
        own_x[0:FIRST] = x_one[...]
        own_x[FIRST:FRAMES] = x_two[...]
        own_g[0:FIRST] = g_one[...]
        own_g[FIRST:FRAMES] = g_two[...]
        for ref in (params, stat_c, stat_d, stat_f, smalls):
            ref[...] = jnp.zeros_like(ref)
        for ref in (band_x, long_g, long_m):
            for start in (0, 160):
                ref[:, start : start + 32, :] = jnp.zeros((FRAMES, 32, ref.shape[2]), BF16)
        for row, ref in enumerate((gain_one, shift_one, bias_one, gain_two, shift_two, bias_two)):
            params[n, row : row + 1, :] = ref[...].astype(F32)
        band_x[:, mine_long, :] = own_x[...]
        long_g[:, mine_long, :] = own_g[:, :, lanes_of(n)]

        barrier = pltpu.get_barrier_semaphore()
        for m in others:
            pl.semaphore_signal(barrier, inc=1, device_id=beside(m), device_id_type=MESH)
        for c in far:
            pl.semaphore_signal(barrier, inc=1, device_id=band_of(c), device_id_type=MESH)
        for sub, (start, stop) in enumerate(((0, FIRST), (FIRST, FRAMES))):
            values = own_x[start:stop].astype(F32).reshape((stop - start) * OWN, CHANNELS)
            total, square = moments(values)
            cuts = [slice(k * SLICE, (k + 1) * SLICE) for k in range(NARROW)]
            t, s = group_merge(
                jnp.concatenate([total[:, cut] for cut in cuts], axis=0),
                jnp.concatenate([square[:, cut] for cut in cuts], axis=0),
                float(values.shape[0]),
            )
            stat_a[n, 8 * sub : 8 * sub + 4, :] = t
            stat_a[n, 8 * sub + 4 : 8 * sub + 8, :] = s
        pl.semaphore_wait(barrier, NARROW - 1 + BANDS - 1)
        to_narrow(stat_a, 0)
        rims_out()
        for m in others:
            send(own_g.at[:, :, lanes_of(m)], long_g.at[:, mine_long, :], g_sem.at[n], beside(m))
            send(params.at[n], params.at[n], p_sem.at[n], beside(m))
        clear_pads(wide_one, wide_two)
        clear_pads(three_one, three_two)

    def xsend():
        for m in (opp, sib):
            send(own_x, band_x.at[:, mine_long, :], x_sem.at[n], beside(m))

    def st0():
        from_narrow(stat_a, 0)
        for sub, count in ((0, 3 * OWN * 16.0), (1, 2 * OWN * 16.0)):
            t, s = merge(
                [stat_a[m, 8 * sub : 8 * sub + 4, :] for m in range(NARROW)],
                [stat_a[m, 8 * sub + 4 : 8 * sub + 8, :] for m in range(NARROW)],
                count,
            )
            stat_b[b, 8 * sub : 8 * sub + 4, :] = t
            stat_b[b, 8 * sub + 4 : 8 * sub + 8, :] = s
        to_bands(stat_b, 1)

    def gown():
        for m in others:
            arrived(long_g.at[:, mine_long, :], g_sem.at[m])
        exchange_rims(long_g, 4)
        g_all[b] = long_g[:, 32:160, :]

    def rim_parts():
        return (
            (band_x.at[0:3, 0:32, :], 0, own_x.at[0:3], below, has_down, has_up, 3),
            (band_x.at[3:5, 16:32, :], 2, own_x.at[3:5, 16:32, :], beyond, pair_down, pair_up, 3),
            (band_x.at[0:3, 160:192, :], 1, own_x.at[0:3], above, has_up, has_down, 0),
            (band_x.at[3:5, 160:176, :], 3, own_x.at[3:5, 0:16, :], beyond, pair_up, pair_down, 0),
        )

    def rims_out():
        for ref, number, own, target, gives, _, owner in rim_parts():
            send(own, ref, halo_sem.at[number], band_of(target), both(gives, n == owner))

    def xh1():
        for ref, number, _, _, _, takes, owner in rim_parts():
            flag = both(takes, n == owner)
            arrived(ref, halo_sem.at[number], flag)
            send(ref, ref, halo_sem.at[number], beside(opp), flag)
            send(ref, ref, halo_sem.at[number], beside(sib), flag)

    def xh2():
        for ref, number, _, _, _, takes, owner in rim_parts():
            flag = both(takes, n == (owner + 2) % 4)
            arrived(ref, halo_sem.at[number], flag)
            send(ref, ref, halo_sem.at[number], beside(sib), flag)

    def xh3():
        for ref, number, _, _, _, takes, owner in rim_parts():
            arrived(ref, halo_sem.at[number], both(takes, n % 2 != owner % 2))

    def xown():
        arrived(band_x.at[:, mine_long, :], x_sem.at[opp])
        theirs = band_x.at[:, rows_of(opp, 32), :]
        send(theirs, theirs, x_sem.at[opp], beside(sib))
        arrived(band_x.at[:, mine_long, :], x_sem.at[sib])
        arrived(band_x.at[:, mine_long, :], x_sem.at[cross])

    def first_hidden(values, sub):
        normed = (values - kept["mean_one"][sub]) * kept["inv_one"][sub]
        return normed, normed * kept["gain_long"] + kept["shift_long"]

    def first_active(f, start, stop):
        _, hidden = first_hidden(band_x[f, start:stop].astype(F32), sub_of(f))
        return (hidden * sigmoid_of(hidden)).astype(BF16)

    def act():
        for m in others:
            arrived(params.at[n], p_sem.at[m])
        from_bands(stat_b, 1)
        one_total, one_square = merge(
            [stat_b[c, 0:4, :] for c in range(BANDS)],
            [stat_b[c, 4:8, :] for c in range(BANDS)],
            3 * BAND * 16.0,
        )
        two_total, two_square = merge(
            [stat_b[b, 8:12, :], stat_b[beyond, 8:12, :]],
            [stat_b[b, 12:16, :], stat_b[beyond, 12:16, :]],
            2 * BAND * 16.0,
        )
        kept["mean_one"] = [
            long_row(one_total / (16.0 * count_one), 0),
            long_row(two_total / (16.0 * count_two), 0),
        ]
        kept["inv_one"] = [
            long_row(lax.rsqrt(one_square / (16.0 * count_one) + EPS), 0),
            long_row(lax.rsqrt(two_square / (16.0 * count_two) + EPS), 0),
        ]
        kept["gain_long"] = jnp.concatenate([params[m, 0:1, :] for m in range(NARROW)], axis=1)
        kept["shift_long"] = jnp.concatenate([params[m, 1:2, :] for m in range(NARROW)], axis=1)
        for f in range(FRAMES):
            active = first_active(f, 32, 160)
            band_a[f, 32:160, :] = active
            for k in range(NARROW):
                cut = slice(k * SLICE, (k + 1) * SLICE)
                act_t1[b, f, lanes_of(place_of(k)), :] = active[:, cut].T

    def lay_out(long):
        for start, stop in ((0, FIRST), (FIRST, FRAMES)):

            @pl.loop(start, stop)
            def _(f, start=start):
                grad_three[f] = three_shifts(long[f], width_of(start))

    def t2():
        await_rims(long_g, 4)
        lay_out(long_g)
        for load in kept["loads"][:3]:
            load.wait()
        conv_backward(grad_three, exit_w, partial, 0)

    def t2c():
        conv_backward(grad_three, exit_w, partial, 2)
        part_send[0] = partial[:, :, lanes_of(sib)].astype(BF16)
        part_send[1] = partial[:, :, lanes_of(cross)].astype(BF16)
        for k in range(2):
            send(part_send.at[k], part_recv.at[k], rs_sem.at[0, k], beside(sib))

    def rs0():
        for k in range(2):
            arrived(part_recv.at[k], rs_sem.at[0, k])
        part_send[2] = (partial[:, :, lanes_of(opp)] + part_recv[1].astype(F32)).astype(BF16)
        send(part_send.at[2], part_recv.at[2], rs_sem.at[0, 2], beside(opp))

    def c1():
        xh3()
        for f in range(FRAMES):
            width = width_of(f)
            up, down = flags(f)
            row = first_active(f, 32 - width, 32)
            band_a[f, 32 - width : 32, :] = jnp.where(up, row, jnp.zeros_like(row))
            row = first_active(f, 160, 160 + width)
            band_a[f, 160 : 160 + width, :] = jnp.where(down, row, jnp.zeros_like(row))
        for load in kept["loads"][3:]:
            load.wait()
        conv_forward(band_a, entry_w, sums, 0)

    def c1c():
        conv_forward(band_a, entry_w, sums, 2)
        for f in range(FRAMES):
            mid[f] = conv_columns(sums, f, width_of(f)) + params[n, 2:3, :]
        for sub, (start, stop) in enumerate(((0, FIRST), (FIRST, FRAMES))):
            values = mid[start:stop].reshape((stop - start) * BAND, SLICE)
            total, square = moments(values)
            t, s = group_merge(total, square, float(values.shape[0]))
            stat_c[b, 2 * sub : 2 * sub + 1, :] = t
            stat_c[b, 2 * sub + 1 : 2 * sub + 2, :] = s
        to_bands(stat_c, 2)

    def s2():
        from_bands(stat_c, 2)
        one_total, one_square = merge(
            [stat_c[c, 0:1, :] for c in range(BANDS)],
            [stat_c[c, 1:2, :] for c in range(BANDS)],
            3 * BAND * 16.0,
        )
        two_total, two_square = merge(
            [stat_c[b, 2:3, :], stat_c[beyond, 2:3, :]],
            [stat_c[b, 3:4, :], stat_c[beyond, 3:4, :]],
            2 * BAND * 16.0,
        )
        mean_two = [one_total / (16.0 * count_one), two_total / (16.0 * count_two)]
        kept["inv_two"] = [
            lax.rsqrt(one_square / (16.0 * count_one) + EPS),
            lax.rsqrt(two_square / (16.0 * count_two) + EPS),
        ]
        kept["gain_own"], kept["shift_own"] = params[n, 3:4, :], params[n, 4:5, :]
        for f in range(FRAMES):
            normed = (mid[f] - mean_two[sub_of(f)]) * kept["inv_two"][sub_of(f)]
            mid[f] = normed
            hidden = normed * kept["gain_own"] + kept["shift_own"]
            act_t2[b, f, lanes_of(place_of(n)), :] = (hidden * sigmoid_of(hidden)).astype(BF16).T

    def gh2():
        arrived(part_recv.at[2], rs_sem.at[0, 2])
        rows_sum = [[0.0, 0.0], [0.0, 0.0]]
        for f in range(FRAMES):
            sub = sub_of(f)
            grad = partial[f, :, lanes_of(n)] + part_recv[0, f].astype(F32) + part_recv[2, f].astype(F32)
            hidden = mid[f] * kept["gain_own"] + kept["shift_own"]
            sigmoid = sigmoid_of(hidden)
            grad = grad * (sigmoid * (1.0 + hidden * (1.0 - sigmoid)))
            grad_two[f] = grad
            rows_sum[sub][0] += jnp.sum(grad, axis=0, keepdims=True)
            rows_sum[sub][1] += jnp.sum(grad * mid[f], axis=0, keepdims=True)
        for sub in range(2):
            stat_d[b, 2 * sub : 2 * sub + 1, :] = rows_sum[sub][0]
            stat_d[b, 2 * sub + 1 : 2 * sub + 2, :] = rows_sum[sub][1]
        own = g_all[b].astype(F32).reshape(FRAMES * BAND, SLICE)
        stat_d[b, 4:5, :] = jnp.sum(own, axis=0, keepdims=True)
        to_bands(stat_d, 3)

    def a2start():
        begin("a2")
        launch([to_opp("a2", b)])

    def a2own():
        o_step("a2", 0, 0)

    def s3():
        from_bands(stat_d, 3)
        gain_own = kept["gain_own"]
        all_rows = [
            functools.reduce(jnp.add, [stat_d[c, r : r + 1, :] for c in range(BANDS)]) for r in range(5)
        ]
        smalls[3:4, :] = all_rows[1] + all_rows[3]
        smalls[4:5, :] = all_rows[0] + all_rows[2]
        smalls[5:6, :] = all_rows[4]
        pair_rows = [stat_d[b, r : r + 1, :] + stat_d[beyond, r : r + 1, :] for r in range(4)]
        p_two = [
            group_sum(gain_own * all_rows[0]) / (16.0 * count_one),
            group_sum(gain_own * pair_rows[2]) / (16.0 * count_two),
        ]
        q_two = [
            group_sum(gain_own * all_rows[1]) / (16.0 * count_one),
            group_sum(gain_own * pair_rows[3]) / (16.0 * count_two),
        ]
        bias_sum = 0.0
        for f in range(FRAMES):
            sub = sub_of(f)
            grad = (grad_two[f] * gain_own - p_two[sub] - mid[f] * q_two[sub]) * kept["inv_two"][sub]
            grad = grad.astype(BF16)
            gm_all[b, f] = grad
            long_m[f, 32:160, :] = grad
            bias_sum = bias_sum + jnp.sum(grad.astype(F32), axis=0, keepdims=True)
        stat_f[b, 16:17, :] = bias_sum
        exchange_rims(long_m, 8)

    def t1():
        await_rims(long_m, 8)
        lay_out(long_m)
        conv_backward(grad_three, entry_w, partial, 0)

    def t1c():
        conv_backward(grad_three, entry_w, partial, 2)
        tail_send[0] = partial[:, rows_of(sib), :].astype(BF16)
        tail_send[1] = partial[:, rows_of(cross), :].astype(BF16)
        for k in range(2):
            send(tail_send.at[k], tail_recv.at[k], rs_sem.at[1, k], beside(sib))

    def rt():
        for k in range(2):
            arrived(tail_recv.at[k], rs_sem.at[1, k])
        tail_send[2] = (partial[:, rows_of(opp), :] + tail_recv[1].astype(F32)).astype(BF16)
        send(tail_send.at[2], tail_recv.at[2], rs_sem.at[1, 2], beside(opp))

    def gh1():
        arrived(tail_recv.at[2], rs_sem.at[1, 2])
        for sub, (start, stop) in enumerate(((0, FIRST), (FIRST, FRAMES))):
            first_sum, second_sum = 0.0, 0.0
            for f in range(start, stop):
                grad = partial[f, mine, :] + tail_recv[0, f].astype(F32) + tail_recv[2, f].astype(F32)
                normed, hidden = first_hidden(own_x[f].astype(F32), sub)
                sigmoid = sigmoid_of(hidden)
                grad = grad * (sigmoid * (1.0 + hidden * (1.0 - sigmoid)))
                grad_one[f] = grad
                first_sum = first_sum + jnp.sum(grad, axis=0, keepdims=True)
                second_sum = second_sum + jnp.sum(grad * normed, axis=0, keepdims=True)
            for k in range(NARROW):
                cut = slice(k * SLICE, (k + 1) * SLICE)
                stat_e[n, 8 * sub + k : 8 * sub + k + 1, :] = first_sum[:, cut]
                stat_e[n, 8 * sub + 4 + k : 8 * sub + 5 + k, :] = second_sum[:, cut]
        to_narrow(stat_e, 4)

    def s4():
        from_narrow(stat_e, 4)
        stat_f[b, 0:16, :] = stat_e[0] + stat_e[1] + stat_e[2] + stat_e[3]
        to_bands(stat_f, 5)

    def s5():
        from_bands(stat_f, 5)
        all_sums = functools.reduce(jnp.add, [stat_f[c] for c in range(BANDS)])
        pair_sums = stat_f[b] + stat_f[beyond]
        few[0, 0:4, :] = all_sums[0:4] + all_sums[8:12]
        few[1, 0:4, :] = all_sums[4:8] + all_sums[12:16]
        smalls[0:1, :] = few[1, pl.ds(n, 1), :]
        smalls[1:2, :] = few[0, pl.ds(n, 1), :]
        smalls[2:3, :] = all_sums[16:17]
        gain_rows = jnp.concatenate([params[m, 0:1, :] for m in range(NARROW)], axis=0)
        p_one = [
            long_row(group_sum(gain_rows * all_sums[0:4]) / (16.0 * count_one), 0),
            long_row(group_sum(gain_rows * pair_sums[8:12]) / (16.0 * count_two), 0),
        ]
        q_one = [
            long_row(group_sum(gain_rows * all_sums[4:8]) / (16.0 * count_one), 0),
            long_row(group_sum(gain_rows * pair_sums[12:16]) / (16.0 * count_two), 0),
        ]
        for f in range(FRAMES):
            sub = sub_of(f)
            normed, _ = first_hidden(own_x[f].astype(F32), sub)
            grad = grad_one[f] * kept["gain_long"] - p_one[sub] - normed * q_one[sub]
            grad = (own_g[f].astype(F32) + grad * kept["inv_one"][sub]).astype(BF16)
            if sub == 0:
                back_one[f] = grad
            else:
                back_two[f - FIRST] = grad

    stores = []

    def store(source, target, number):
        copy = pltpu.make_async_copy(source, target, store_sem.at[number])
        copy.start()
        stores.append(copy)

    def prepa(number):
        first = 2 * pairs_by_distance[number]
        await_sib("a2", first)
        await_sib("a2", first + 1)

    def pad(name, number, array, one, two):
        pair = pairs_by_distance[number]
        c = 2 * pair + 1 - y
        arrived(block(name, c, n), sem(name, c, 0))
        pad_pair(array, one, two, pair)

    def padg(number):
        pad("g", number, g_all, wide_one, wide_two)

    def c2():
        @pl.loop(0, NARROW)
        def _(k):
            cut = lanes_of(k)
            rows = lanes_of(place_of(k))
            for f in range(FRAMES):
                width = width_of(f)
                up, down = flags(f)
                band_a[f, 32:160, cut] = act_t2[b, f, rows, :].T
                row = act_t2[b - (b + 7) // 8, f, rows, :].T[BAND - width : BAND]
                band_a[f, 32 - width : 32, cut] = jnp.where(up, row, jnp.zeros_like(row))
                row = act_t2[b + (14 - b) // 8, f, rows, :].T[0:width]
                band_a[f, 160 : 160 + width, cut] = jnp.where(down, row, jnp.zeros_like(row))

        conv_forward(band_a, exit_w, sums, 0)

    def c2c():
        conv_forward(band_a, exit_w, sums, 2)
        for f in range(FRAMES):
            total = conv_columns(sums, f, width_of(f)) + params[n, 5:6, :]
            total = total + band_x[f, 32:160, lanes_of(n)].astype(F32)
            out_send[f] = total.astype(BF16)
        for m in others:
            send(out_send.at[0:3, rows_of(m), :], out_one.at[:, :, lanes_of(n)], o_sem.at[0, n], beside(m))
            send(out_send.at[3:5, rows_of(m), :], out_two.at[:, :, lanes_of(n)], o_sem.at[1, n], beside(m))
        out_one[:, :, lanes_of(n)] = out_send[0:3, mine, :]
        out_two[:, :, lanes_of(n)] = out_send[3:5, mine, :]

    def out():
        for m in others:
            arrived(out_one.at[:, :, lanes_of(m)], o_sem.at[0, m])
            arrived(out_two.at[:, :, lanes_of(m)], o_sem.at[1, m])

    def wx(number, place, group):
        i = PARTS[place]
        taps = TAP_GROUPS[group]
        pair = pairs_by_distance[number]
        pair_weight_terms(act_t2, wide_one, wide_two, pair, i, taps, exit_sum, number == 0)
        if number == 3 and group == len(TAP_GROUPS) - 1:
            cut = slice(9 * i, 9 * i + 9)
            store(exit_sum.at[cut], exit_grad.at[cut], 6 + i)

    def prepx(number):
        first = 2 * pairs_by_distance[number]
        if number == 0:
            await_sib("x", beyond)
        else:
            await_sib("x", first)
            await_sib("x", first + 1)
        store(act_t1.at[pl.ds(first, 2)], act_out.at[pl.ds(first, 2)], number)

    def padm(number):
        pad("m", number, gm_all, three_one, three_two)
        if number == 3:
            store(three_one, wide_one_out, 4)
            store(three_two, wide_two_out, 5)

    def fin():
        reap(len(sends))
        for copy in stores:
            copy.wait()

    backward = lambda weights, part: lambda: conv_backward(grad_three, weights, partial, part)
    forward = lambda weights, part: lambda: conv_forward(band_a, weights, sums, part)
    steps = {
        "prep": prep, "xsend": xsend, "st0": st0, "gown": gown, "xown": xown, "xh1": xh1, "xh2": xh2, "act": act,
        "T2": t2, "T2b": backward(exit_w, 1), "T2c": t2c, "rs0": rs0,
        "C1": c1, "C1b": forward(entry_w, 1), "C1c": c1c,
        "S2": s2, "gh2": gh2, "a2start": a2start, "a2own": a2own, "S3": s3,
        "T1": t1, "T1b": backward(entry_w, 1), "T1c": t1c, "rt": rt, "gh1": gh1, "S4": s4, "S5": s5,
        "C2": c2, "C2b": forward(exit_w, 1), "C2c": c2c, "out": out,
        "padg": padg, "padm": padm, "fin": fin,
        "gstart": lambda: begin("g"),
        "mstart": lambda: begin("m"),
        "xbulk": lambda: begin("x"),
        "z": z_step, "y": y_step, "o": o_step, "wx": wx, "prepx": prepx, "prepa": prepa,
    }
    before = 0
    for number, item in enumerate(ORDER):
        if number in REAPS:
            count, before = before, len(sends) - before
            reap(count)
        word, *rest = item.split()
        steps[word](*[int(r) if r.isdigit() else r for r in rest])


def run_block(args):
    vmem = pl.BlockSpec(memory_space=pltpu.VMEM)
    hbm = pl.BlockSpec(memory_space=pl.ANY)
    dma = pltpu.SemaphoreType.DMA
    shape = jax.ShapeDtypeStruct
    everyone = (BANDS, FRAMES, CHANNELS, BAND)
    wide_one = (FIRST, 34 * 32, 3 * SLICE)
    wide_two = (FRAMES - FIRST, 4, 18 * 16, 3 * SLICE)
    return pl.pallas_call(
        block_kernel,
        out_shape=(
            shape((FIRST, OWN, CHANNELS), BF16),
            shape((FRAMES - FIRST, OWN, CHANNELS), BF16),
            shape((FIRST, OWN, CHANNELS), BF16),
            shape((FRAMES - FIRST, OWN, CHANNELS), BF16),
            shape((8, SLICE), F32),
            shape(everyone, BF16),
            shape(wide_one, BF16),
            shape(wide_two, BF16),
            shape((27, CHANNELS, SLICE), F32),
        ),
        in_specs=[vmem] * 10 + [hbm] * 2,
        out_specs=(vmem,) * 5 + (hbm,) * 4,
        scratch_shapes=[
            pltpu.VMEM(everyone, BF16),
            pltpu.VMEM(everyone, BF16),
            pltpu.VMEM((BANDS, FRAMES, BAND, SLICE), BF16),
            pltpu.VMEM((BANDS, FRAMES, BAND, SLICE), BF16),
            pltpu.VMEM(wide_one, BF16),
            pltpu.VMEM(wide_two, BF16),
            pltpu.VMEM(wide_one, BF16),
            pltpu.VMEM(wide_two, BF16),
            pltpu.VMEM((27, CHANNELS, SLICE), F32),
            pltpu.VMEM((9, CHANNELS, 3 * SLICE), BF16),
            pltpu.VMEM((9, CHANNELS, 3 * SLICE), BF16),
            pltpu.VMEM((FRAMES, OWN, CHANNELS), BF16),
            pltpu.VMEM((FRAMES, OWN, CHANNELS), BF16),
            pltpu.VMEM((FRAMES, LONG, CHANNELS), BF16),
            pltpu.VMEM((FRAMES, LONG, CHANNELS), BF16),
            pltpu.VMEM((FRAMES, LONG, SLICE), BF16),
            pltpu.VMEM((FRAMES, LONG, SLICE), BF16),
            pltpu.VMEM((NARROW, 8, SLICE), F32),
            pltpu.VMEM((NARROW, 16, SLICE), F32),
            pltpu.VMEM((BANDS, 16, SLICE), F32),
            pltpu.VMEM((BANDS, 8, SLICE), F32),
            pltpu.VMEM((BANDS, 8, SLICE), F32),
            pltpu.VMEM((NARROW, 16, SLICE), F32),
            pltpu.VMEM((BANDS, 24, SLICE), F32),
            pltpu.VMEM((2, 8, SLICE), F32),
            pltpu.VMEM((FRAMES, BAND, 3 * SLICE), F32),
            pltpu.VMEM((FRAMES, BAND, CHANNELS), F32),
            pltpu.VMEM((FRAMES, LONG, 3 * SLICE), BF16),
            pltpu.VMEM((FRAMES, BAND, SLICE), F32),
            pltpu.VMEM((FRAMES, BAND, SLICE), F32),
            pltpu.VMEM((FRAMES, OWN, CHANNELS), F32),
            pltpu.VMEM((3, FRAMES, BAND, SLICE), BF16),
            pltpu.VMEM((3, FRAMES, BAND, SLICE), BF16),
            pltpu.VMEM((3, FRAMES, OWN, CHANNELS), BF16),
            pltpu.VMEM((3, FRAMES, OWN, CHANNELS), BF16),
            pltpu.VMEM((FRAMES, BAND, SLICE), BF16),
            dma((2, 3)),
            dma((288,)),
            dma((NARROW,)),
            dma((NARROW,)),
            dma((NARROW,)),
            dma((12,)),
            dma((6, BANDS)),
            dma((BANDS,)),
            dma((BANDS,)),
            dma((BANDS, 3)),
            dma((BANDS, 3)),
            dma((2, 3)),
            dma((2, NARROW)),
            dma((9,)),
        ],
        compiler_params=pltpu.CompilerParams(
            collective_id=0, has_side_effects=True, vmem_limit_bytes=62 * 1024 * 1024
        ),
        cost_estimate=pl.CostEstimate(flops=20 * 10**9, bytes_accessed=3 * 10**7, transcendentals=0),
        name="block",
    )(*args)


def last_kernel(act_hbm, one_hbm, two_hbm, exit_hbm, smalls, *refs):
    rows, (entry_out, exit_out, *vectors), rest = refs[:4], refs[4:12], refs[12:]
    row_outs, (act_t, wide_one, wide_two, entry_sum, exit_sum, load_sem, store_sem) = rest[:4], rest[4:]

    loads = []
    for f in range(FRAMES):
        first = pltpu.make_async_copy(act_hbm.at[:, f], act_t.at[:, f], load_sem.at[f])
        if f < FIRST:
            second = pltpu.make_async_copy(one_hbm.at[f], wide_one.at[f], load_sem.at[FRAMES + f])
        else:
            place = f - FIRST
            second = pltpu.make_async_copy(two_hbm.at[place], wide_two.at[place], load_sem.at[FRAMES + f])
        first.start()
        second.start()
        loads.append((first, second))
    through = pltpu.make_async_copy(exit_hbm, exit_sum, load_sem.at[2 * FRAMES])
    through.start()
    for row, ref in enumerate(vectors):
        ref[...] = smalls[row : row + 1, :]
    for source, target in zip(rows, row_outs):
        target[...] = source[...]

    stores = []

    def store(source, target):
        copy = pltpu.make_async_copy(source, target, store_sem.at[len(stores)])
        copy.start()
        stores.append(copy)

    def terms(i, pairs, fresh, last):
        for group in TAP_GROUPS[:4]:
            weight_terms(act_t, wide_one, wide_two, i, pairs, group, entry_sum, fresh)
            if last:
                taps = slice(9 * i + group[0], 9 * i + group[-1] + 1)
                store(entry_sum.at[taps], entry_out.at[taps])

    for parts, pairs in ((loads[:2], PAIRS[1][:2]), (loads[2:], PAIRS[1][2:])):
        for first, second in parts:
            first.wait()
            second.wait()
        terms(1, pairs, pairs[0][0] == 0, pairs[-1][0] == FRAMES - 1)
    through.wait()
    store(exit_sum, exit_out)
    terms(0, PAIRS[0], True, True)
    seen = set()
    for s in range(FRAMES):
        meets = [(i, t) for i in range(3) for other, t in PAIRS[i] if other == s]
        right = jnp.concatenate([tap_rows(wide_one, wide_two, t, 8) for _, t in meets], axis=1)
        left = jnp.concatenate([act_t[c, s] for c in range(BANDS)], axis=1)
        result = jnp.dot(left, right, preferred_element_type=F32)
        for place, (i, _) in enumerate(meets):
            part = result[:, place * SLICE : (place + 1) * SLICE]
            store_taps(entry_sum, [9 * i + 8], part, i not in seen)
            seen.add(i)
    for i in range(3):
        store(entry_sum.at[9 * i + 8 : 9 * i + 9], entry_out.at[9 * i + 8 : 9 * i + 9])
    terms(2, PAIRS[2], True, True)
    for copy in stores:
        copy.wait()


def run_last(act, wide_one, wide_two, smalls, rows, exit_grad):
    vmem = pl.BlockSpec(memory_space=pltpu.VMEM)
    hbm = pl.BlockSpec(memory_space=pl.ANY)
    shape = jax.ShapeDtypeStruct
    taps = shape((27, CHANNELS, SLICE), F32)
    return pl.pallas_call(
        last_kernel,
        out_shape=(taps, taps, *[shape((1, SLICE), F32)] * 6, *[shape(r.shape, r.dtype) for r in rows]),
        in_specs=[hbm] * 4 + [vmem] * 5,
        out_specs=(hbm, hbm, *[vmem] * 10),
        scratch_shapes=[
            pltpu.VMEM(act.shape, BF16),
            pltpu.VMEM(wide_one.shape, BF16),
            pltpu.VMEM(wide_two.shape, BF16),
            pltpu.VMEM(taps.shape, F32),
            pltpu.VMEM(taps.shape, F32),
            pltpu.SemaphoreType.DMA((2 * FRAMES + 1,)),
            pltpu.SemaphoreType.DMA((16,)),
        ],
        compiler_params=pltpu.CompilerParams(vmem_limit_bytes=60 * 1024 * 1024),
        cost_estimate=pl.CostEstimate(flops=14 * 10**9, bytes_accessed=35 * 10**6, transcendentals=0),
        name="last",
    )(act, wide_one, wide_two, exit_grad, smalls, *rows)


def local(
    first_input,
    second_input,
    first_cotangent,
    second_cotangent,
    entry_gain,
    entry_shift,
    entry_kernel,
    entry_bias,
    exit_gain,
    exit_shift,
    exit_kernel,
    exit_bias,
):
    def rows(values):
        return values.reshape(values.shape[0], OWN, CHANNELS)

    vectors = [
        v.reshape(1, SLICE) for v in (entry_gain, entry_shift, entry_bias, exit_gain, exit_shift, exit_bias)
    ]
    taps = [k.reshape(9, 3, CHANNELS, SLICE) for k in (entry_kernel, exit_kernel)]
    *home, smalls, act_one, wide_one, wide_two, exit_grad = run_block(
        [
            rows(first_input),
            rows(second_input),
            rows(first_cotangent),
            rows(second_cotangent),
            *vectors,
            *taps,
        ]
    )
    entry_grad, exit_grad, *rest = run_last(act_one, wide_one, wide_two, smalls, home, exit_grad)
    small, (out_one, out_two, back_one, back_two) = rest[:6], rest[6:]
    totals = (*small, entry_grad, exit_grad)
    groups = lax.axis_size("wide") // BANDS
    if groups > 1:
        totals = tuple(lax.psum(t, "wide") / BANDS for t in totals)
    *small, entry_grad, exit_grad = totals
    small = [t.reshape(SLICE) for t in small]
    return (
        out_one.reshape(first_input.shape),
        out_two.reshape(second_input.shape),
        back_one.reshape(first_input.shape),
        back_two.reshape(second_input.shape),
        small[0],
        small[1],
        entry_grad,
        small[2],
        small[3],
        small[4],
        exit_grad,
        small[5],
    )


def solution(mesh):
    banded = P(None, ("wide", "narrow"), None, None)
    vector = P("narrow")
    kernel = P(None, None, "narrow")
    return jax.shard_map(
        local,
        mesh=mesh,
        in_specs=(banded,) * 4 + (vector, vector, kernel, vector) * 2,
        out_specs=(banded,) * 4 + (vector, vector, kernel, vector) * 2,
        check_vma=False,
    )
```

time: 1210 us -> 115 us (0.10)
  blocking collectives: 847 us -> 0 us
  local copies, waits for them, and re-layouts: 146 us -> 0 us
  matrix products: 135 us -> 0 us
  Pallas kernels: 0 us -> 114 us
  starting transfers between devices: 37.2 us -> 0 us
  between operations: 18 us -> 0.86 us
  other arithmetic: 13 us -> 0 us
    psum x7 -> x0, blocking collectives: 804 us -> none  [the longest x1 547 us: local(): totals = lax.psum(shares, 'wide')]
    unnamed x365 -> x0, local copies, waits for them, and re-layouts: 137 us -> none
    dot_general x12 -> x0, matrix products: 135 us -> none  [the longest x4 58 us: kernel_grad(): lax.dot_general(patches, grad_rows, (((0,), (0,)), ((), ())), preferred_e...]
    pallas_call x0 -> x2, Pallas kernels: none -> 114 us  [the longest x1 94.6 us: run_block(): pl.pallas_call(block_kernel, out_shape=(shape((FIRST, OWN, CHANNELS), BF1...]
    all_gather x6 -> x0, blocking collectives: 37.2 us -> none  [the longest x1 9.31 us: local(): lax.all_gather(exit_bias, 'narrow', axis=0, tiled=True)]
    ppermute x16 -> x0, starting transfers between devices: 37.1 us -> none  [the longest x8 26.4 us: extended_2(): lax.ppermute(lax.slice_in_dim(block, block.shape[dim] - width, None, axis...]
  transfers between devices with their start and end apart: 20 -> 0, of which waited for: 0 -> 0; matrix products, arithmetic and copies ran while one was open for 15% -> 0% of each run, Pallas kernels for 0% -> 0%
where the time goes in v1:
time: 115 us
  Pallas kernels  114 us (99%)
    pallas_call x1, Pallas kernels, run_block(): pl.pallas_call(block_kernel, out_shape=(shape((FIRST, OWN, CHANNELS), BF1...  94.6 us
    pallas_call x1, Pallas kernels, run_last(): pl.pallas_call(last_kernel, out_shape=(taps, taps, *[shape((1, SLICE), F3...  19.2 us

profile of v1, /device:TPU:0, one launch (start us, length us, event | category | flops | bytes accessed | tf_op | source)
XLA Modules:
  0.0 114.6 jit_solution(3087403886549074402)
XLA Ops:
  0.6 94.6 %block.1 = (bf16[3,32,512]{2,1,0:T(8,128)(2,1)}, bf16[2,32,512]{2,1,0:T(8,128)(2,1)}, bf16[3,32,512]{2,1,0:T(8,128)(2,1)}, bf16[2,32,512]{2,1,0:T(8,128)(2,1)}, ...) custom-call(bf16[3,32,512]{2,1,0:T(8,128)(2,1)} %bitcast.28, ...), custom_call_target="tpu_custom_call" | custom-call | flops 20000000000 | bytes 30000000 | tf_op jit(solution)/shard_map/block/pallas_call | solution.py:1048
  95.2 19.2 %last.1 = (f32[27,512,128]{2,1,0:T(8,128)}, f32[27,512,128]{2,1,0:T(8,128)}, f32[1,128]{1,0:T(1,128)}, f32[1,128]{1,0:T(1,128)}, f32[1,128]{1,0:T(1,128)}, /*ind...) custom-call(bf16[8,5,512,128]{3,2,1,0:T(8,128)(2,1)} %get-tuple-elem, ...), custom_call_target="tpu_custom_call" | custom-call | flops 14000000000 | bytes 35000000 | tf_op jit(solution)/shard_map/last/pallas_call | solution.py:1189

commit v2 on v1

--- a/solution.py
+++ b/solution.py
@@ -43,8 +43,8 @@
     "st0",
     "xh1",
     "gown",
+    "xsend",
     "gstart",
-    "xsend",
     "xh2",
     "T2",
     "T2b",
@@ -53,133 +53,133 @@
     "act",
     "T2c",
     "C1",
-    "z g 2",
+    "xbulk",
+    "rs0",
     "C1b",
     "C1c",
-    "rs0",
     "S2",
     "a2start",
+    "y a2 0",
+    "z g 2",
+    "a2own",
+    "gh2",
+    "z a2 1",
+    "o a2 0 1",
+    "padg 0",
+    "padg 1",
+    "padg 2",
+    "S3",
     "z g 3",
-    "padg 0",
-    "z a2 1",
-    "padg 1",
-    "gh2",
-    "S3",
-    "padg 2",
-    "a2own",
-    "padg 3",
-    "y a2 0",
-    "xbulk",
-    "T1",
-    "y a2 1",
-    "o a2 0 1",
-    "T1b",
-    "o a2 1 0",
+    "prepa 0",
     "z a2 2",
-    "prepa 0",
     "wx 0 0 0",
     "wx 0 0 1",
     "wx 0 0 2",
     "wx 0 0 3",
+    "o a2 1 0",
     "wx 0 0 4",
+    "wx 0 1 0",
+    "wx 0 1 1",
     "z x 1",
-    "T1c",
-    "wx 0 1 0",
-    "z a2 3",
-    "wx 0 1 1",
+    "y a2 1",
     "wx 0 1 2",
     "wx 0 1 3",
     "wx 0 1 4",
     "wx 0 2 0",
+    "z a2 3",
+    "T1",
+    "T1b",
     "wx 0 2 1",
+    "T1c",
     "wx 0 2 2",
+    "wx 0 2 3",
+    "mstart",
     "o a2 1 1",
     "y a2 2",
-    "wx 0 2 3",
     "wx 0 2 4",
-    "mstart",
+    "padg 3",
     "o a2 2 0",
+    "z x 2",
     "prepa 1",
     "wx 1 0 0",
     "wx 1 0 1",
     "wx 1 0 2",
+    "rt",
     "wx 1 0 3",
-    "rt",
     "wx 1 0 4",
     "wx 1 1 0",
     "wx 1 1 1",
     "wx 1 1 2",
     "wx 1 1 3",
-    "z x 2",
-    "y a2 3",
     "wx 1 1 4",
+    "o a2 3 0",
     "wx 1 2 0",
     "wx 1 2 1",
+    "wx 1 2 2",
     "o a2 2 1",
+    "wx 1 2 3",
     "y x 0",
-    "wx 1 2 2",
-    "wx 1 2 3",
+    "y a2 3",
     "wx 1 2 4",
+    "z m 1",
+    "prepa 2",
+    "C2",
     "y x 1",
-    "prepa 2",
     "wx 2 0 0",
-    "C2",
     "wx 2 0 1",
-    "z m 1",
+    "gh1",
     "wx 2 0 2",
-    "o a2 3 0",
     "wx 2 0 3",
     "wx 2 0 4",
+    "z x 3",
     "wx 2 1 0",
+    "C2b",
+    "padm 0",
+    "y x 2",
     "wx 2 1 1",
-    "padm 0",
+    "o a2 3 1",
+    "z m 2",
     "wx 2 1 2",
     "wx 2 1 3",
     "wx 2 1 4",
-    "z x 3",
     "wx 2 2 0",
     "wx 2 2 1",
     "wx 2 2 2",
     "wx 2 2 3",
+    "prepa 3",
     "wx 2 2 4",
-    "y x 2",
-    "o a2 3 1",
-    "z m 2",
-    "C2b",
-    "gh1",
+    "wx 3 0 0",
+    "o x 0 1",
+    "wx 3 0 1",
+    "wx 3 0 2",
+    "y x 3",
     "o x 1 1",
-    "C2c",
-    "prepa 3",
-    "wx 3 0 0",
-    "wx 3 0 1",
-    "y x 3",
-    "o x 0 1",
+    "padm 1",
+    "prepx 0",
     "z m 3",
-    "wx 3 0 2",
-    "S4",
     "wx 3 0 3",
     "wx 3 0 4",
     "wx 3 1 0",
     "wx 3 1 1",
     "wx 3 1 2",
     "wx 3 1 3",
+    "wx 3 1 4",
     "o x 2 1",
-    "padm 1",
-    "wx 3 1 4",
+    "S4",
     "wx 3 2 0",
     "wx 3 2 1",
-    "padm 2",
-    "prepx 0",
+    "wx 3 2 2",
+    "o x 3 1",
     "prepx 1",
     "prepx 2",
-    "o x 3 1",
-    "wx 3 2 2",
+    "C2c",
+    "prepx 3",
     "wx 3 2 3",
+    "wx 3 2 4",
+    "padm 2",
+    "padm 3",
+    "S5",
     "out",
-    "wx 3 2 4",
-    "S5",
-    "padm 3",
-    "prepx 3",
     "fin",
 )
 REAPS = (47, 71, 94, 118, 136)
@@ -577,6 +577,13 @@
         arrived(ref.at[0:3, 160:192, :], halo_sem.at[first_sem + 1], has_down)
         arrived(ref.at[3:5, 16:32, :], halo_sem.at[first_sem + 2], pair_up)
         arrived(ref.at[3:5, 160:176, :], halo_sem.at[first_sem + 3], pair_down)
+
+    stores = []
+
+    def store(source, target, number):
+        copy = pltpu.make_async_copy(source, target, store_sem.at[number])
+        copy.start()
+        stores.append(copy)
 
     kept = {}
     count_one = 3 * BAND * BANDS
@@ -634,6 +641,9 @@
         clear_pads(three_one, three_two)
 
     def xsend():
+        for number, start in enumerate((0, three_one.shape[1] - 32)):
+            rows = slice(start, start + 32)
+            store(three_one.at[:, rows, :], wide_one_out.at[:, rows, :], 12 + number)
         for m in (opp, sib):
             send(own_x, band_x.at[:, mine_long, :], x_sem.at[n], beside(m))
 
@@ -731,11 +741,8 @@
                 act_t1[b, f, lanes_of(place_of(k)), :] = active[:, cut].T
 
     def lay_out(long):
-        for start, stop in ((0, FIRST), (FIRST, FRAMES)):
-
-            @pl.loop(start, stop)
-            def _(f, start=start):
-                grad_three[f] = three_shifts(long[f], width_of(start))
+        for f in range(FRAMES):
+            grad_three[f] = three_shifts(long[f], width_of(f))
 
     def t2():
         await_rims(long_g, 4)
@@ -930,13 +937,6 @@
             else:
                 back_two[f - FIRST] = grad
 
-    stores = []
-
-    def store(source, target, number):
-        copy = pltpu.make_async_copy(source, target, store_sem.at[number])
-        copy.start()
-        stores.append(copy)
-
     def prepa(number):
         first = 2 * pairs_by_distance[number]
         await_sib("a2", first)
@@ -991,7 +991,7 @@
         pair_weight_terms(act_t2, wide_one, wide_two, pair, i, taps, exit_sum, number == 0)
         if number == 3 and group == len(TAP_GROUPS) - 1:
             cut = slice(9 * i, 9 * i + 9)
-            store(exit_sum.at[cut], exit_grad.at[cut], 6 + i)
+            store(exit_sum.at[cut], exit_grad.at[cut], 14 + i)
 
     def prepx(number):
         first = 2 * pairs_by_distance[number]
@@ -1004,9 +1004,10 @@
 
     def padm(number):
         pad("m", number, gm_all, three_one, three_two)
-        if number == 3:
-            store(three_one, wide_one_out, 4)
-            store(three_two, wide_two_out, 5)
+        pair = pairs_by_distance[number]
+        rows = pl.ds(pl.multiple_of(32 + pair * 2 * BAND, 32), 2 * BAND)
+        store(three_one.at[:, rows, :], wide_one_out.at[:, rows, :], 4 + number)
+        store(three_two.at[:, pair], wide_two_out.at[:, pair], 8 + number)
 
     def fin():
         reap(len(sends))
@@ -1110,7 +1111,7 @@
             dma((BANDS, 3)),
             dma((2, 3)),
             dma((2, NARROW)),
-            dma((9,)),
+            dma((17,)),
         ],
         compiler_params=pltpu.CompilerParams(
             collective_id=0, has_side_effects=True, vmem_limit_bytes=62 * 1024 * 1024

time: 115 us -> 112 us (0.974)
  Pallas kernels: 114 us -> 111 us
    pallas_call x1, Pallas kernels: 94.6 us -> 91.6 us  [run_block(): pl.pallas_call(block_kernel, out_shape=(shape((FIRST, OWN, CHANNELS), BF1...]
where the time goes in v2:
time: 112 us
  Pallas kernels  111 us (99%)
    pallas_call x1, Pallas kernels, run_block(): pl.pallas_call(block_kernel, out_shape=(shape((FIRST, OWN, CHANNELS), BF1...  91.6 us
    pallas_call x1, Pallas kernels, run_last(): pl.pallas_call(last_kernel, out_shape=(taps, taps, *[shape((1, SLICE), F3...  19.2 us

profile of v2, /device:TPU:0, one launch (start us, length us, event | category | flops | bytes accessed | tf_op | source)
XLA Modules:
  0.0 111.6 jit_solution(2271323447416394029)
XLA Ops:
  0.6 91.6 %block.1 = (bf16[3,32,512]{2,1,0:T(8,128)(2,1)}, bf16[2,32,512]{2,1,0:T(8,128)(2,1)}, bf16[3,32,512]{2,1,0:T(8,128)(2,1)}, bf16[2,32,512]{2,1,0:T(8,128)(2,1)}, ...) custom-call(bf16[3,32,512]{2,1,0:T(8,128)(2,1)} %bitcast.28, ...), custom_call_target="tpu_custom_call" | custom-call | flops 20000000000 | bytes 30000000 | tf_op jit(solution)/shard_map/block/pallas_call | solution.py:1049
  92.2 19.2 %last.1 = (f32[27,512,128]{2,1,0:T(8,128)}, f32[27,512,128]{2,1,0:T(8,128)}, f32[1,128]{1,0:T(1,128)}, f32[1,128]{1,0:T(1,128)}, f32[1,128]{1,0:T(1,128)}, /*ind...) custom-call(bf16[8,5,512,128]{3,2,1,0:T(8,128)(2,1)} %get-tuple-elem, ...), custom_call_target="tpu_custom_call" | custom-call | flops 14000000000 | bytes 35000000 | tf_op jit(solution)/shard_map/last/pallas_call | solution.py:1190

commit v3 on v2

--- a/solution.py
+++ b/solution.py
@@ -41,139 +41,139 @@
 ORDER = (
     "prep",
     "st0",
+    "xsend",
     "xh1",
     "gown",
-    "xsend",
     "gstart",
-    "xh2",
     "T2",
     "T2b",
     "z g 1",
+    "xh2",
     "xown",
     "act",
+    "xbulk",
     "T2c",
     "C1",
-    "xbulk",
-    "rs0",
     "C1b",
     "C1c",
+    "z g 2",
+    "rs0",
     "S2",
     "a2start",
+    "gh2",
+    "padg 0",
     "y a2 0",
-    "z g 2",
     "a2own",
-    "gh2",
-    "z a2 1",
-    "o a2 0 1",
-    "padg 0",
+    "S3",
     "padg 1",
     "padg 2",
-    "S3",
-    "z g 3",
+    "z a2 1",
+    "T1",
+    "mstart",
+    "o a2 0 1",
+    "T1b",
+    "T1c",
+    "y a2 1",
     "prepa 0",
     "z a2 2",
     "wx 0 0 0",
     "wx 0 0 1",
     "wx 0 0 2",
+    "o a2 1 0",
+    "z g 3",
+    "z x 1",
     "wx 0 0 3",
-    "o a2 1 0",
     "wx 0 0 4",
     "wx 0 1 0",
     "wx 0 1 1",
-    "z x 1",
-    "y a2 1",
     "wx 0 1 2",
     "wx 0 1 3",
     "wx 0 1 4",
     "wx 0 2 0",
-    "z a2 3",
-    "T1",
-    "T1b",
     "wx 0 2 1",
-    "T1c",
     "wx 0 2 2",
-    "wx 0 2 3",
-    "mstart",
+    "padm 0",
     "o a2 1 1",
     "y a2 2",
+    "wx 0 2 3",
     "wx 0 2 4",
-    "padg 3",
-    "o a2 2 0",
-    "z x 2",
+    "z a2 3",
     "prepa 1",
     "wx 1 0 0",
     "wx 1 0 1",
     "wx 1 0 2",
+    "wx 1 0 3",
+    "z m 1",
+    "wx 1 0 4",
+    "padg 3",
+    "wx 1 1 0",
     "rt",
-    "wx 1 0 3",
-    "wx 1 0 4",
-    "wx 1 1 0",
     "wx 1 1 1",
     "wx 1 1 2",
+    "o a2 2 0",
     "wx 1 1 3",
     "wx 1 1 4",
-    "o a2 3 0",
     "wx 1 2 0",
+    "z x 2",
     "wx 1 2 1",
     "wx 1 2 2",
     "o a2 2 1",
+    "y a2 3",
+    "prepa 2",
+    "y x 0",
+    "C2",
     "wx 1 2 3",
-    "y x 0",
-    "y a2 3",
     "wx 1 2 4",
-    "z m 1",
-    "prepa 2",
-    "C2",
+    "wx 2 0 0",
     "y x 1",
-    "wx 2 0 0",
     "wx 2 0 1",
-    "gh1",
     "wx 2 0 2",
+    "o a2 3 0",
     "wx 2 0 3",
     "wx 2 0 4",
+    "wx 2 1 0",
+    "wx 2 1 1",
+    "wx 2 1 2",
     "z x 3",
-    "wx 2 1 0",
+    "gh1",
+    "o a2 3 1",
+    "wx 2 1 3",
     "C2b",
-    "padm 0",
+    "z m 2",
+    "prepa 3",
     "y x 2",
-    "wx 2 1 1",
-    "o a2 3 1",
-    "z m 2",
-    "wx 2 1 2",
-    "wx 2 1 3",
+    "o x 0 1",
     "wx 2 1 4",
+    "padm 1",
     "wx 2 2 0",
     "wx 2 2 1",
     "wx 2 2 2",
     "wx 2 2 3",
-    "prepa 3",
     "wx 2 2 4",
     "wx 3 0 0",
-    "o x 0 1",
+    "y x 3",
     "wx 3 0 1",
     "wx 3 0 2",
-    "y x 3",
     "o x 1 1",
-    "padm 1",
+    "wx 3 0 3",
+    "z m 3",
+    "wx 3 0 4",
+    "S4",
+    "C2c",
     "prepx 0",
-    "z m 3",
-    "wx 3 0 3",
-    "wx 3 0 4",
+    "prepx 1",
+    "o x 2 1",
     "wx 3 1 0",
     "wx 3 1 1",
+    "o x 3 1",
     "wx 3 1 2",
     "wx 3 1 3",
     "wx 3 1 4",
-    "o x 2 1",
-    "S4",
     "wx 3 2 0",
+    "prepx 2",
+    "prepx 3",
     "wx 3 2 1",
     "wx 3 2 2",
-    "o x 3 1",
-    "prepx 1",
-    "prepx 2",
-    "C2c",
-    "prepx 3",
     "wx 3 2 3",
     "wx 3 2 4",
     "padm 2",

time: 112 us -> 112 us (level)
  no operation moved by 1% of the time
where the time goes in v3:
time: 112 us
  Pallas kernels  111 us (99%)
    pallas_call x1, Pallas kernels, run_block(): pl.pallas_call(block_kernel, out_shape=(shape((FIRST, OWN, CHANNELS), BF1...  91.8 us
    pallas_call x1, Pallas kernels, run_last(): pl.pallas_call(last_kernel, out_shape=(taps, taps, *[shape((1, SLICE), F3...  19.2 us

profile of v3, /device:TPU:0, one launch (start us, length us, event | category | flops | bytes accessed | tf_op | source)
XLA Modules:
  0.0 111.9 jit_solution(3088770312234598118)
XLA Ops:
  0.6 91.8 %block.1 = (bf16[3,32,512]{2,1,0:T(8,128)(2,1)}, bf16[2,32,512]{2,1,0:T(8,128)(2,1)}, bf16[3,32,512]{2,1,0:T(8,128)(2,1)}, bf16[2,32,512]{2,1,0:T(8,128)(2,1)}, ...) custom-call(bf16[3,32,512]{2,1,0:T(8,128)(2,1)} %bitcast.28, ...), custom_call_target="tpu_custom_call" | custom-call | flops 20000000000 | bytes 30000000 | tf_op jit(solution)/shard_map/block/pallas_call | solution.py:1049
  92.5 19.2 %last.1 = (f32[27,512,128]{2,1,0:T(8,128)}, f32[27,512,128]{2,1,0:T(8,128)}, f32[1,128]{1,0:T(1,128)}, f32[1,128]{1,0:T(1,128)}, f32[1,128]{1,0:T(1,128)}, /*ind...) custom-call(bf16[8,5,512,128]{3,2,1,0:T(8,128)(2,1)} %get-tuple-elem, ...), custom_call_target="tpu_custom_call" | custom-call | flops 14000000000 | bytes 35000000 | tf_op jit(solution)/shard_map/last/pallas_call | solution.py:1190

commit v4 on v3

--- a/solution.py
+++ b/solution.py
@@ -42,144 +42,144 @@
     "prep",
     "st0",
     "xsend",
-    "xh1",
     "gown",
     "gstart",
+    "xh1",
     "T2",
-    "T2b",
+    "xown",
     "z g 1",
     "xh2",
-    "xown",
     "act",
-    "xbulk",
-    "T2c",
     "C1",
     "C1b",
     "C1c",
     "z g 2",
-    "rs0",
+    "T2b",
     "S2",
     "a2start",
-    "gh2",
+    "T2c",
+    "rs0",
+    "a2own",
+    "z g 3",
+    "xbulk",
+    "y a2 0",
     "padg 0",
-    "y a2 0",
-    "a2own",
-    "S3",
     "padg 1",
     "padg 2",
     "z a2 1",
-    "T1",
-    "mstart",
     "o a2 0 1",
-    "T1b",
-    "T1c",
-    "y a2 1",
+    "padg 3",
+    "gh2",
     "prepa 0",
-    "z a2 2",
     "wx 0 0 0",
     "wx 0 0 1",
+    "y a2 1",
+    "z a2 2",
     "wx 0 0 2",
-    "o a2 1 0",
-    "z g 3",
-    "z x 1",
     "wx 0 0 3",
     "wx 0 0 4",
+    "S3",
     "wx 0 1 0",
     "wx 0 1 1",
     "wx 0 1 2",
+    "z x 1",
     "wx 0 1 3",
+    "z a2 3",
+    "o a2 1 0",
     "wx 0 1 4",
+    "mstart",
     "wx 0 2 0",
     "wx 0 2 1",
     "wx 0 2 2",
-    "padm 0",
-    "o a2 1 1",
-    "y a2 2",
     "wx 0 2 3",
     "wx 0 2 4",
-    "z a2 3",
+    "y a2 2",
+    "T1",
+    "y x 0",
+    "o a2 1 1",
+    "T1b",
+    "T1c",
     "prepa 1",
     "wx 1 0 0",
     "wx 1 0 1",
     "wx 1 0 2",
     "wx 1 0 3",
-    "z m 1",
     "wx 1 0 4",
-    "padg 3",
     "wx 1 1 0",
-    "rt",
     "wx 1 1 1",
     "wx 1 1 2",
     "o a2 2 0",
     "wx 1 1 3",
     "wx 1 1 4",
+    "z m 1",
+    "o a2 2 1",
     "wx 1 2 0",
-    "z x 2",
+    "rt",
     "wx 1 2 1",
     "wx 1 2 2",
-    "o a2 2 1",
-    "y a2 3",
+    "wx 1 2 3",
+    "z x 2",
+    "wx 1 2 4",
     "prepa 2",
-    "y x 0",
-    "C2",
-    "wx 1 2 3",
-    "wx 1 2 4",
     "wx 2 0 0",
-    "y x 1",
     "wx 2 0 1",
     "wx 2 0 2",
-    "o a2 3 0",
+    "o x 0 1",
     "wx 2 0 3",
     "wx 2 0 4",
+    "y x 1",
+    "C2",
+    "y a2 3",
+    "C2b",
+    "o a2 3 0",
     "wx 2 1 0",
+    "C2c",
     "wx 2 1 1",
-    "wx 2 1 2",
     "z x 3",
     "gh1",
+    "wx 2 1 2",
+    "wx 2 1 3",
+    "wx 2 1 4",
     "o a2 3 1",
-    "wx 2 1 3",
-    "C2b",
+    "y x 2",
     "z m 2",
-    "prepa 3",
-    "y x 2",
-    "o x 0 1",
-    "wx 2 1 4",
-    "padm 1",
     "wx 2 2 0",
     "wx 2 2 1",
     "wx 2 2 2",
     "wx 2 2 3",
+    "padm 0",
+    "padm 1",
     "wx 2 2 4",
+    "S4",
+    "o x 1 1",
+    "y x 3",
+    "prepa 3",
     "wx 3 0 0",
-    "y x 3",
     "wx 3 0 1",
     "wx 3 0 2",
-    "o x 1 1",
+    "z m 3",
+    "prepx 0",
     "wx 3 0 3",
-    "z m 3",
+    "prepx 1",
     "wx 3 0 4",
-    "S4",
-    "C2c",
-    "prepx 0",
-    "prepx 1",
     "o x 2 1",
     "wx 3 1 0",
+    "out",
     "wx 3 1 1",
-    "o x 3 1",
     "wx 3 1 2",
     "wx 3 1 3",
+    "o x 3 1",
     "wx 3 1 4",
     "wx 3 2 0",
-    "prepx 2",
-    "prepx 3",
     "wx 3 2 1",
     "wx 3 2 2",
+    "prepx 2",
     "wx 3 2 3",
+    "prepx 3",
     "wx 3 2 4",
     "padm 2",
     "padm 3",
     "S5",
-    "out",
     "fin",
 )
 REAPS = (47, 71, 94, 118, 136)

time: 112 us -> 111 us (level)
  no operation moved by 1% of the time
where the time goes in v4:
time: 111 us
  Pallas kernels  110 us (99%)
    pallas_call x1, Pallas kernels, run_block(): pl.pallas_call(block_kernel, out_shape=(shape((FIRST, OWN, CHANNELS), BF1...  91.2 us
    pallas_call x1, Pallas kernels, run_last(): pl.pallas_call(last_kernel, out_shape=(taps, taps, *[shape((1, SLICE), F3...  19.2 us

profile of v4, /device:TPU:0, one launch (start us, length us, event | category | flops | bytes accessed | tf_op | source)
XLA Modules:
  0.0 111.2 jit_solution(4920671174529178184)
XLA Ops:
  0.6 91.2 %block.1 = (bf16[3,32,512]{2,1,0:T(8,128)(2,1)}, bf16[2,32,512]{2,1,0:T(8,128)(2,1)}, bf16[3,32,512]{2,1,0:T(8,128)(2,1)}, bf16[2,32,512]{2,1,0:T(8,128)(2,1)}, ...) custom-call(bf16[3,32,512]{2,1,0:T(8,128)(2,1)} %bitcast.28, ...), custom_call_target="tpu_custom_call" | custom-call | flops 20000000000 | bytes 30000000 | tf_op jit(solution)/shard_map/block/pallas_call | solution.py:1049
  91.8 19.2 %last.1 = (f32[27,512,128]{2,1,0:T(8,128)}, f32[27,512,128]{2,1,0:T(8,128)}, f32[1,128]{1,0:T(1,128)}, f32[1,128]{1,0:T(1,128)}, f32[1,128]{1,0:T(1,128)}, /*ind...) custom-call(bf16[8,5,512,128]{3,2,1,0:T(8,128)(2,1)} %get-tuple-elem, ...), custom_call_target="tpu_custom_call" | custom-call | flops 14000000000 | bytes 35000000 | tf_op jit(solution)/shard_map/last/pallas_call | solution.py:1190
